TPU v7x, 512 devices: a whole 4x4x16 slice. The times are simulated.
512 devices in a mesh: rows: 64 (over x, z_lo, y), grp: 8 (over z_hi, core).
Axes of the slice: x: 4, y: 4, z: 16 (z_hi: 4, z_lo: 4; z = z_hi * 4 + z_lo), core: 2. Of those that a mesh axis runs over, the one named last changes fastest.
Arguments:
- latent_features: bfloat16 [8, 96, 5, 128, 128], P('grp', None, None, 'rows'), may hold values from -6 to 6
- conv_weight: bfloat16 [27, 96, 96], replicated, may hold values from -0.125 to 0.125
- conv_bias: float32 [96], replicated, may hold values from -3 to 3
- out_weight: bfloat16 [27, 96, 3], replicated, may hold values from -0.125 to 0.125
- out_bias: float32 [3], replicated, may hold values from -3 to 3
- target_frames: bfloat16 [8, 3, 5, 128, 128], P('grp', None, None, 'rows'), may hold values from -96 to 96
Outputs:
- decoded: bfloat16 [8, 3, 5, 128, 128], P('grp', None, None, 'rows')
- grad_conv_weight: float32 [27, 96, 96], replicated
- grad_conv_bias: float32 [96], replicated
- grad_out_weight: float32 [27, 96, 3], replicated
- grad_out_bias: float32 [3], replicated
All inputs are finite; a program needn't handle non-finite values.
Results may differ from a plain program's by a relative error of at most 0.005.
Values may be sent and summed in bfloat16 or wider, within the bound.
No kernel may reach another device: no remote copies, remote signals or barrier semaphores. Data moves between devices by JAX's collectives and lax.ppermute only.
A program may use at most 64 MiB of HBM per device.

v0:
```python
import math

import jax
import jax.numpy as jnp
from jax import lax
from jax.sharding import PartitionSpec as P


def extended(cells, sides, width):
    for axis, dim in sides:
        count = lax.axis_size(axis)
        ends = count - 1
        head = lax.slice_in_dim(cells, 0, width, axis=dim)
        tail = lax.slice_in_dim(cells, cells.shape[dim] - width, cells.shape[dim], axis=dim)
        cells = jnp.concatenate(
            [
                lax.ppermute(tail, axis, [(i, (i + 1) % count) for i in range(ends)]),
                cells,
                lax.ppermute(head, axis, [((i + 1) % count, i) for i in range(ends)]),
            ],
            axis=dim,
        )
    return cells


def tap_conv(padded, weight, frames, rows_out, columns, flipped):
    summed = None
    for kernel_tap in range(27):
        depth_off = kernel_tap // 9
        row_off = kernel_tap // 3 % 3
        col_off = kernel_tap % 3
        if flipped:
            starts = (0, 2 - depth_off, 2 - row_off, 2 - col_off)
            matrix = weight[kernel_tap].T
        else:
            starts = (0, depth_off, row_off, col_off)
            matrix = weight[kernel_tap]
        window = lax.slice(
            padded,
            starts,
            (padded.shape[0], starts[1] + frames, starts[2] + rows_out, starts[3] + columns),
        )
        product = lax.dot_general(
            matrix, window, (((0,), (0,)), ((), ())), preferred_element_type=jnp.float32
        )
        summed = product if summed is None else summed + product
    return summed


def tap_grads(padded, grad, frames, rows_out, columns):
    results = []
    for kernel_tap in range(27):
        depth_off = kernel_tap // 9
        row_off = kernel_tap // 3 % 3
        col_off = kernel_tap % 3
        window = lax.slice(
            padded,
            (0, depth_off, row_off, col_off),
            (padded.shape[0], depth_off + frames, row_off + rows_out, col_off + columns),
        )
        results.append(
            lax.dot_general(
                window, grad, (((1, 2, 3), (1, 2, 3)), ((), ())), preferred_element_type=jnp.float32
            )
        )
    return jnp.stack(results)


def local(latent_features, conv_weight, conv_bias, out_weight, out_bias, target_frames):
    latent = latent_features[0]
    target = target_frames[0]
    channels, frames, slab_rows, columns = latent.shape
    row_count = lax.axis_size("rows")
    frame_rows = slab_rows * row_count
    loss_scale = 1.0 / math.sqrt(
        3 * latent_features.shape[0] * lax.axis_size("grp") * frames * frame_rows * columns
    )
    bias_conv = conv_bias[:, None, None, None]
    rimmed = extended(latent, (("rows", 2),), 1)
    padded_in = jnp.pad(rimmed, ((0, 0), (2, 0), (0, 0), (1, 1)))
    pre_act = tap_conv(padded_in, conv_weight, frames, slab_rows, columns, False) + bias_conv
    sig_pre = jax.nn.sigmoid(pre_act)
    hidden = (pre_act * sig_pre).astype(jnp.bfloat16)
    hidden_rimmed = extended(hidden, (("rows", 2),), 1)
    padded_hidden = jnp.pad(hidden_rimmed, ((0, 0), (2, 0), (0, 0), (1, 1)))
    out_pre = (
        tap_conv(padded_hidden, out_weight, frames, slab_rows, columns, False)
        + out_bias[:, None, None, None]
    )
    decoded = out_pre.astype(jnp.bfloat16)
    grad_frames = ((decoded.astype(jnp.float32) - target.astype(jnp.float32)) * loss_scale).astype(
        jnp.bfloat16
    )
    grad_rimmed = extended(grad_frames, (("rows", 2),), 1)
    padded_grad = jnp.pad(grad_rimmed, ((0, 0), (0, 2), (0, 0), (1, 1)))
    backed = tap_conv(padded_grad, out_weight, frames, slab_rows, columns, True)
    grad_hidden = (backed * sig_pre * (1.0 + pre_act * (1.0 - sig_pre))).astype(jnp.bfloat16)
    grad_conv = tap_grads(padded_in, grad_hidden, frames, slab_rows, columns)
    grad_cbias = jnp.sum(grad_hidden.astype(jnp.float32), axis=(1, 2, 3))
    grad_outw = tap_grads(padded_hidden, grad_frames, frames, slab_rows, columns)
    grad_obias = jnp.sum(grad_frames.astype(jnp.float32), axis=(1, 2, 3))
    grad_conv, grad_outw, grad_cbias, grad_obias = lax.psum(
        (grad_conv, grad_outw, grad_cbias, grad_obias), ("rows", "grp")
    )
    return (decoded[None], grad_conv, grad_cbias, grad_outw, grad_obias)


def solution(mesh):
    return jax.shard_map(
        local,
        mesh=mesh,
        in_specs=(
            P("grp", None, None, "rows", None),
            P(),
            P(),
            P(),
            P(),
            P("grp", None, None, "rows", None),
        ),
        out_specs=(P("grp", None, None, "rows", None), P(), P(), P(), P()),
        check_vma=False,
    )
```

profile of v0, /device:TPU:1, one launch (start us, length us, event | category | flops | bytes accessed | tf_op | source)
XLA Modules:
  0.0 568.4 jit_solution(146418236949081604)
XLA Ops:
  7.2 1.0 copy.323
  8.2 4.2 collective-permute-start
  12.4 1.3 collective-permute-start.1
  13.7 1.2 fusion.295
  15.0 3.0 collective-permute-done.1
  18.0 0.5 fusion.13
  18.6 0.3 convolution_bitcast_fusion.10
  19.1 0.3 convolution_bitcast_fusion.7
  20.3 0.3 fusion.238
  20.6 0.3 fusion.241
  21.2 0.3 fusion.247
  21.5 0.3 fusion.250
  22.0 0.3 fusion.256
  22.3 0.3 fusion.259
  22.9 0.3 fusion.265
  23.2 0.3 fusion.268
  23.8 0.3 fusion.274
  24.1 0.3 fusion.277
  24.4 0.3 convolution_bitcast_fusion.2
  25.0 0.8 fusion.57
  25.8 0.3 fusion.21
  26.4 0.4 multiply_convert_fusion
  26.8 3.5 collective-permute-start.2
  30.3 1.5 collective-permute-start.3
  32.2 3.8 collective-permute-done.3
  36.0 0.5 fusion.10
  41.7 0.4 convert_reduce_fusion.1
  47.8 4.6 collective-permute-start.4
  52.5 1.5 collective-permute-start.5
  54.2 2.6 collective-permute-done.5
  58.7 0.3 convolution_add_fusion.16
  59.3 0.3 convolution_add_fusion.14
  59.6 0.3 convolution_add_fusion.13
  60.2 0.3 convolution_add_fusion.11
  60.6 0.3 convolution_add_fusion.10
  61.2 0.3 convolution_add_fusion.8
  61.5 0.3 convolution_add_fusion.7
  62.1 0.3 convolution_add_fusion.5
  62.4 0.3 convolution_add_fusion.4
  63.0 0.3 convolution_add_fusion.2
  63.3 0.3 fusion.32
  64.5 0.5 convert_reduce_fusion
  71.9 1.1 copy-done.1
  73.1 0.7 copy.68
  74.2 124.0 %all-reduce.3 = (f32[96]{0:T(128)}, f32[27,96,3]{1,2,0:T(4,128)S(1)}, f32[3]{0:T(128)}) all-reduce(f32[96]{0:T(128)S(1)} %get-tuple-element.51, f32[27,96,3]{1,2,0:T(4,128)S(1)} %fusion.114, f32[3]{0:T(128)S(1)} %get-tuple-element.13), channel_id=1, replica_groups=mesh['rows'=64,'grp'=8] {'rows','grp'}, use_global_device_ids=true, to_apply=%region_2.3 | all-reduce | flops 7875 | bytes 63000 | tf_op jit(solution)/shard_map/psum | solution.py:102
  198.2 0.6 copy.69
  198.8 360.3 %all-reduce.6.cloned.1.call-done = f32[27,96,96]{2,1,0:T(8,128)} async-done(((f32[27,96,96]{2,1,0:T(8,128)}), f32[27,96,96]{2,1,0:T(8,128)}) %all-reduce.6.cloned.1.call-update) | async-done | bytes 995344 | tf_op jit(solution)/shard_map/psum | solution.py:102
  559.1 2.5 copy.377
  (129 shorter events, 25.8 us)
Async XLA Ops:
  7.2 7.8 %copy-start.3 = (bf16[27,96,3]{1,0,2:T(8,128)(2,1)S(1)}, bf16[27,96,3]{1,0,2:T(8,128)(2,1)}, u32[]{:S(2)}) copy-start(bf16[27,96,3]{1,0,2:T(8,128)(2,1)} %param.9) | copy-start | bytes 46660
  7.2 551.9 %all-reduce.6.cloned.1.call-start = ((), (), s32[]{:S(2)}) async-start(), calls=%async_computation | async-start | bytes 2654208 | tf_op jit(solution)/shard_map/psum | solution.py:102
  8.2 10.3 %copy-start.2 = (bf16[27,96,96]{2,1,0:T(8,128)(2,1)S(1)}, bf16[27,96,96]{2,1,0:T(8,128)(2,1)}, u32[]{:S(2)}) copy-start(bf16[27,96,96]{2,1,0:T(8,128)(2,1)} %param.7) | copy-start | bytes 1492996
  8.2 6.8 %collective-permute-start = (bf16[96,5,1,128]{3,0,2,1:T(8,128)(2,1)S(1)}, bf16[96,5,1,128]{3,0,2,1:T(8,128)(2,1)S(1)}, u32[]{:S(2)}, u32[]{:S(2)}) collective-permute-start(bf16[96,5,1,128]{3,0,2,1:T(8,128)(2,1)S(1)} %get-tuple-element.17), channel_id=1, source_target_pairs={{0,8},{8,16},{16,24},{24,32},{32,40},{40,48},{48,56},{56,64},{64,7... | collective-permute-start | bytes 368648 | tf_op jit(solution)/shard_map/ppermute | solution.py:17
  12.4 5.6 collective-permute-start.1
  25.8 0.7 copy-start.5
  26.8 5.3 collective-permute-start.2
  30.3 5.6 collective-permute-start.3
  40.6 1.2 copy-start.4
  40.6 1.2 copy-start.6
  47.8 6.4 %collective-permute-start.4 = (bf16[3,5,1,128]{3,0,2,1:T(4,128)(2,1)S(1)}, bf16[3,5,1,128]{3,0,2,1:T(4,128)(2,1)S(1)}, u32[]{:S(2)}, u32[]{:S(2)}) collective-permute-start(bf16[3,5,1,128]{3,0,2,1:T(4,128)(2,1)S(1)} %get-tuple-element.46), channel_id=1, source_target_pairs={{0,8},{8,16},{16,24},{24,32},{32,40},{40,48},{48,56},{56,64},{64,7... | collective-permute-start | bytes 11528 | tf_op jit(solution)/shard_map/ppermute | solution.py:17
  52.5 4.4 collective-permute-start.5
  69.4 1.3 copy-start
  71.9 1.1 copy-start.1
Sparse Core Ops, SparseCore 0:
  73.1 485.9 all-reduce.5
where the time goes:
time: 569 us; the launch traced here: 568 us
  waiting for transfers between devices  370 us (65%)
  blocking collectives  124 us (22%)
  matrix products  36.2 us (6%)
  starting transfers between devices  16.6 us (3%)
  between operations  14.7 us (3%)
  local copies, waits for them, and re-layouts  5.98 us (1%)
    psum x1, waiting for transfers between devices, local(): lax.psum((grad_conv, grad_outw, grad_cbias, grad_obias), ('rows', 'grp'))  360 us
    psum x1, blocking collectives, local(): lax.psum((grad_conv, grad_outw, grad_cbias, grad_obias), ('rows', 'grp'))  124 us
    dot_general x81, matrix products, tap_conv(): lax.dot_general(matrix, window, (((0,), (0,)), ((), ())), preferred_eleme...  23.2 us
    dot_general x54, matrix products, tap_grads(): lax.dot_general(window, grad, (((1, 2, 3), (1, 2, 3)), ((), ())), preferr...  13 us
    ppermute x3, starting transfers between devices, extended(): lax.ppermute(tail, axis, [(i, (i + 1) % count) for i in range(ends)])  12.3 us
  transfers between devices with their start and end apart: 7, of which 5 were waited for; matrix products, arithmetic and copies ran while one was open for 1% of the time, Pallas kernels for 0%

commit v1 on v0

v1 whole, which is shorter than its diff:
```python
import functools
import math

import jax
import jax.numpy as jnp
from jax import lax
from jax.experimental import pallas as pl
from jax.experimental.pallas import tpu as pltpu
from jax.sharding import Mesh, PartitionSpec as P

BF = jnp.bfloat16
F32 = jnp.float32
C = 96
F = 5
W = 128
TAPS = 27
TPAD = 28
OPAD = 8
GROWS = TPAD * OPAD
HR = 4
FW = HR * W
POS = F * FW
KT = 9 * C
NW = TAPS * C
MAIN = 1920
TAIL = NW - MAIN
ROWS = 2048
EDGE_AXES = ("x", "zl", "y")
PLANE = ("x", "y", "c")
DEPTH = ("zl", "zh")


def nt(a, b):
    return lax.dot_general(a, b, (((1,), (1,)), ((), ())), preferred_element_type=F32)


def nn(a, b):
    return lax.dot_general(a, b, (((1,), (0,)), ((), ())), preferred_element_type=F32)


def tn(a, b):
    return lax.dot_general(a, b, (((0,), (0,)), ((), ())), preferred_element_type=F32)


def shifted(v, lane, by):
    if by == 0:
        return v
    if by > 0:
        return jnp.where(lane < W - 1, pltpu.roll(v, W - 1, 1), 0.0)
    return jnp.where(lane > 0, pltpu.roll(v, 1, 1), 0.0)


def device_kernel(
    n_rows, scale,
    own_ref, pair_ref, wt_ref, cb_ref, wo_ref, ob_ref, tgt_ref,
    dec_ref, pay_ref,
    q_ref, hid_ref, fac_ref, y_ref, g_ref, gh_ref, main_ref,
):
    row_id = (lax.axis_index("x") * lax.axis_size("zl") + lax.axis_index("zl")) * lax.axis_size(
        "y"
    ) + lax.axis_index("y")
    odd = lax.rem(row_id, 2)
    first = row_id == 0
    last = row_id == n_rows - 1
    lane96 = lax.broadcasted_iota(jnp.int32, (C, W), 1)
    lane8 = lax.broadcasted_iota(jnp.int32, (OPAD, W), 1)

    for g in range(F):
        for r in range(6):
            if r < 2:
                tile = pair_ref[1 - odd, g, r]
            elif r < 4:
                tile = own_ref[g, r - 2]
            else:
                tile = pair_ref[odd, g, r - 4]
            wide = tile.astype(F32)
            for kj in range(3):
                piece = tile if kj == 1 else shifted(wide, lane96, kj - 1).astype(BF)
                for ki in range(3):
                    i = r - ki
                    if 0 <= i < HR:
                        base = (ki * 3 + kj) * C
                        q_ref[base : base + C, g * FW + i * W : g * FW + (i + 1) * W] = piece

    srow = lax.broadcasted_iota(jnp.int32, (C, GROWS), 0)
    scol = lax.broadcasted_iota(jnp.int32, (C, GROWS), 1)
    pick = ((srow // 32 == scol % OPAD) & (srow % 32 == scol // OPAD)).astype(F32).astype(BF)
    wo = wo_ref[...]
    wo8 = tn(pick, wo).astype(BF)
    wo8t = tn(wo, pick).astype(BF)

    col = lax.broadcasted_iota(jnp.int32, (1, FW), 1)
    outside = ((col < W) & first) | ((col >= 3 * W) & last)
    keep = jnp.where(outside, 0.0, 1.0)
    for f in range(F):
        pre = None
        for kt in range(3):
            g = f + kt - 2
            if g < 0:
                continue
            part = nn(wt_ref[:, kt * KT : (kt + 1) * KT], q_ref[:, g * FW : (g + 1) * FW])
            pre = part if pre is None else pre + part
        pre = pre + cb_ref[...]
        sig = jax.nn.sigmoid(pre)
        hid = (pre * sig * keep).astype(BF)
        hid_ref[:, f * FW : (f + 1) * FW] = hid
        fac_ref[:, f * FW : (f + 1) * FW] = sig * (1.0 + pre * (1.0 - sig)) * keep
        y_ref[:, f * FW : (f + 1) * FW] = nn(wo8, hid)

    grads = {}
    obsum = jnp.zeros((OPAD, W), F32)
    for f in range(F):
        for i in range(2):
            dec = None
            for kj in range(3):
                z = None
                for kt in range(3):
                    g = f + kt - 2
                    if g < 0:
                        continue
                    for ki in range(3):
                        t = kt * 9 + ki * 3 + kj
                        at = g * FW + (i + ki) * W
                        v = y_ref[t * OPAD : (t + 1) * OPAD, at : at + W]
                        z = v if z is None else z + v
                z = shifted(z, lane8, kj - 1)
                dec = z if dec is None else dec + z
            dec = (dec + ob_ref[...]).astype(BF)
            at = (f * 2 + i) * W
            dec_ref[:, at : at + W] = dec.astype(F32)
            gf = ((dec.astype(F32) - tgt_ref[:, at : at + W]) * scale).astype(BF).astype(F32)
            obsum = obsum + gf
            for kj in range(3):
                grads[f, i, kj] = shifted(gf, lane8, 1 - kj)

    none = jnp.zeros((OPAD, W), F32)
    for g in range(F):
        for i in range(HR):
            parts = []
            for t in range(TPAD):
                kt, ki, kj = t // 9, t // 3 % 3, t % 3
                parts.append(grads.get((g + 2 - kt, i - ki, kj), none) if t < TAPS else none)
            at = g * FW + i * W
            for p in range(TPAD // 2):
                both = jnp.concatenate(parts[2 * p : 2 * p + 2], axis=0).astype(BF)
                g_ref[p * 16 : (p + 1) * 16, at : at + W] = both

    gh_ref[C:, :] = jnp.zeros((W - C, POS), BF)
    for f in range(F):
        back = nn(wo8t, g_ref[:, f * FW : (f + 1) * FW])
        gh_ref[:C, f * FW : (f + 1) * FW] = (back * fac_ref[:, f * FW : (f + 1) * FW]).astype(BF)

    for kt in range(3):
        main_ref[kt * KT : (kt + 1) * KT, :] = nt(
            q_ref[:, : (3 + kt) * FW], gh_ref[:, (2 - kt) * FW :]
        )
    gow = nt(g_ref[...], hid_ref[...]).astype(BF)
    gow = nn(pick, gow)
    bias = nt(jnp.ones((OPAD, POS), BF), gh_ref[...])
    obias = jnp.broadcast_to(jnp.sum(obsum, axis=1, keepdims=True), (OPAD, W))

    for k in range(3):
        lo, hi = k * TAIL, (k + 1) * TAIL
        tail = pltpu.roll(main_ref[MAIN:, :], 96 - 32 * k, 1)
        if hi <= MAIN:
            head = main_ref[lo:hi, :]
        else:
            head = jnp.concatenate(
                [main_ref[lo:MAIN, :], jnp.pad(gow, ((0, 0), (0, W - C)))], axis=0
            )
        lane = lax.broadcasted_iota(jnp.int32, (TAIL, W), 1)
        pay_ref[lo:hi, :] = jnp.where(lane < C, head, tail).astype(BF)
    for at, v in ((2016, bias), (2032, obias)):
        top = v.astype(BF).astype(F32)
        pay_ref[at : at + 16, :] = jnp.concatenate([top, v - top], axis=0).astype(BF)


def split_sums(total, is_last):
    out = total.astype(BF)
    fixed = []
    for at in (32, 48):
        whole = total[at : at + 8] + total[at + 8 : at + 16]
        top = whole.astype(BF).astype(F32)
        fixed += [top, whole - top]
    special = jnp.concatenate([total[:32]] + fixed, axis=0).astype(BF)
    return jnp.where(is_last, special, out)


def sum_kernel(copies, in_ref, out_ref):
    total = in_ref[0].astype(F32)
    for k in range(1, in_ref.shape[0]):
        total = total + in_ref[k].astype(F32)
    index = (lax.axis_index("x") * lax.axis_size("y") + lax.axis_index("y")) * lax.axis_size(
        "c"
    ) + lax.axis_index("c")
    count = lax.axis_size("x") * lax.axis_size("y") * lax.axis_size("c")
    res = split_sums(total, index == count - 1)
    for k in range(copies):
        out_ref[k] = res


def unpack_kernel(in_ref, gw_ref, gb_ref, go_ref, gob_ref):
    gw_ref[:MAIN, :] = in_ref[:MAIN, :C].astype(F32)
    lane = lax.broadcasted_iota(jnp.int32, (TAIL, W), 1)
    tail = None
    for k in range(3):
        v = pltpu.roll(in_ref[k * TAIL : (k + 1) * TAIL, :].astype(F32), 32 + 32 * k, 1)
        tail = v if tail is None else jnp.where(lane < 32 * k, tail, v)
    gw_ref[MAIN:, :] = tail[:, :C]
    gow = in_ref[MAIN : MAIN + 96, :].astype(F32)
    for o in range(3):
        go_ref[o] = gow[o * 32 : o * 32 + TAPS, :C]
    sums = in_ref[2016:2048, :].astype(F32)
    gb_ref[...] = (sums[0:8] + sums[8:16])[0:1, :C]
    ob = sums[16:24] + sums[24:32]
    r8 = lax.broadcasted_iota(jnp.int32, (OPAD, W), 0)
    l8 = lax.broadcasted_iota(jnp.int32, (OPAD, W), 1)
    gob_ref[...] = jnp.sum(jnp.where(r8 == l8, ob, 0.0), axis=0, keepdims=True)


VM = functools.partial(pl.BlockSpec, memory_space=pltpu.VMEM)
LIMIT = 48 * 1024 * 1024


def local(latent_features, conv_weight, conv_bias, out_weight, out_bias, target_frames):
    sizes = [lax.axis_size(a) for a in EDGE_AXES]
    n_rows = sizes[0] * sizes[1] * sizes[2]
    clips = lax.axis_size("zh") * lax.axis_size("c")
    scale = 1.0 / math.sqrt(3 * clips * F * 2 * n_rows * W)

    own = jnp.transpose(latent_features[0], (1, 2, 0, 3))
    near = [(i, i ^ 1) for i in range(n_rows)]
    far = [(i, ((i + 1) ^ 1) - 1) for i in range(1, n_rows - 1)]
    pair = jnp.stack([lax.ppermute(own, EDGE_AXES, near), lax.ppermute(own, EDGE_AXES, far)])

    wt = jnp.transpose(conv_weight, (2, 0, 1)).reshape(C, NW)
    wo = jnp.pad(jnp.transpose(out_weight, (2, 0, 1)), ((0, 0), (0, 5), (0, 0))).reshape(C, C)
    ob = jnp.pad(out_bias[:, None], ((0, 5), (0, 0)))
    tgt = jnp.pad(target_frames[0].reshape(3, F * 2 * W).astype(F32), ((0, 5), (0, 0)))

    dec, packed = pl.pallas_call(
        functools.partial(device_kernel, n_rows, scale),
        out_shape=(
            jax.ShapeDtypeStruct((OPAD, F * 2 * W), F32),
            jax.ShapeDtypeStruct((ROWS, W), BF),
        ),
        in_specs=[VM()] * 7,
        out_specs=(VM(), VM()),
        scratch_shapes=[
            pltpu.VMEM((KT, POS), BF),
            pltpu.VMEM((C, POS), BF),
            pltpu.VMEM((C, POS), F32),
            pltpu.VMEM((GROWS, POS), F32),
            pltpu.VMEM((GROWS, POS), BF),
            pltpu.VMEM((W, POS), BF),
            pltpu.VMEM((NW, W), F32),
        ],
        compiler_params=pltpu.CompilerParams(vmem_limit_bytes=LIMIT),
        name="device_part",
    )(own, pair, wt, conv_bias[:, None], wo, ob, tgt)

    plane = lax.axis_size("x") * lax.axis_size("y") * lax.axis_size("c")
    depth = lax.axis_size("zl") * lax.axis_size("zh")
    chunk = ROWS // plane

    def summed(parts, copies):
        return pl.pallas_call(
            functools.partial(sum_kernel, copies),
            out_shape=jax.ShapeDtypeStruct((copies, chunk, W), BF),
            in_specs=[VM()],
            out_specs=VM(),
            name="sum_parts",
        )(parts)

    parts = lax.all_to_all(packed.reshape(plane, chunk, W), PLANE, 0, 0)
    parts = lax.all_to_all(summed(parts, depth), DEPTH, 0, 0)
    parts = lax.all_to_all(summed(parts, plane), PLANE, 0, 0)

    gw, gb, go, gob = pl.pallas_call(
        unpack_kernel,
        out_shape=(
            jax.ShapeDtypeStruct((NW, C), F32),
            jax.ShapeDtypeStruct((1, C), F32),
            jax.ShapeDtypeStruct((3, TAPS, C), F32),
            jax.ShapeDtypeStruct((1, W), F32),
        ),
        in_specs=[VM()],
        out_specs=(VM(),) * 4,
        name="unpack",
    )(parts.reshape(ROWS, W))
    decoded = dec[:3].astype(BF).reshape(1, 3, F, 2, W)
    return (
        decoded,
        gw.reshape(TAPS, C, C),
        gb.reshape(C),
        jnp.transpose(go, (1, 2, 0)),
        gob[0, :3],
    )


def solution(mesh):
    split = Mesh(mesh.devices.reshape(4, 4, 4, 4, 2), ("x", "zl", "y", "zh", "c"))
    frames = P(("zh", "c"), None, None, EDGE_AXES, None)
    return jax.shard_map(
        local,
        mesh=split,
        in_specs=(frames, P(), P(), P(), P(), frames),
        out_specs=(frames, P(), P(), P(), P()),
        check_vma=False,
    )
```

time: 569 us -> 101 us (0.18)
  the two profiles are of different devices: /device:TPU:1 before, /device:TPU:33 now
where the time goes in v1:
time: 101 us; the launch traced here: 100 us
  blocking collectives  52.2 us (52%)
  waiting for transfers between devices  13.6 us (13%)
  Pallas kernels  13.2 us (13%)
  starting transfers between devices  13.1 us (13%)
  local copies, waits for them, and re-layouts  7.15 us (7%)
    all_to_all x1, blocking collectives, local(): parts = lax.all_to_all(summed(parts, depth), DEPTH, 0, 0)  32.9 us
    all_to_all x1, blocking collectives, local(): parts = lax.all_to_all(packed.reshape(plane, chunk, W), PLANE, 0, 0)  19.3 us
    all_to_all x1, waiting for transfers between devices, local(): parts = lax.all_to_all(summed(parts, plane), PLANE, 0, 0)  11.1 us
    pallas_call x1, Pallas kernels, local(): pl.pallas_call(functools.partial(device_kernel, n_rows, scale), out_shape...  7.13 us
    all_to_all x1, starting transfers between devices, local(): parts = lax.all_to_all(summed(parts, plane), PLANE, 0, 0)  6.71 us
    ppermute x1, starting transfers between devices, local(): lax.ppermute(own, EDGE_AXES, far)  4.19 us
    pallas_call x2, Pallas kernels, summed(): pl.pallas_call(functools.partial(sum_kernel, copies), out_shape=jax.Shape...  3.7 us
    pallas_call x1, Pallas kernels, local(): pl.pallas_call(unpack_kernel, out_shape=(jax.ShapeDtypeStruct((NW, C), F3...  2.36 us
  transfers between devices with their start and end apart: 3, of which 3 were waited for; matrix products, arithmetic and copies ran while one was open for 4% of the time, Pallas kernels for 0%

profile of v1, /device:TPU:33, one launch (start us, length us, event | category | flops | bytes accessed | tf_op | source)
XLA Modules:
  0.0 100.1 jit_solution(5537163949487838651)
XLA Ops:
  0.6 0.0 copy-start.1
  0.6 1.0 copy.20
  1.6 4.2 %collective-permute-start.1 = (bf16[5,2,96,128]{3,2,1,0:T(8,128)(2,1)S(1)}, bf16[5,2,96,128]{3,2,1,0:T(8,128)(2,1)S(1)}, u32[]{:S(2)}, u32[]{:S(2)}) collective-permute-start(bf16[5,2,96,128]{3,2,1,0:T(8,128)(2,1)S(1)} %bitcast.21), channel_id=1, source_target_pairs={{8,16},{16,8},{24,32},{32,24},{40,48},{48,40},{56,64},{64,56},{72,... | collective-permute-start | bytes 737288 | tf_op jit(solution)/shard_map/ppermute | solution.py:234
  5.8 2.2 %collective-permute-start = (bf16[5,2,96,128]{3,2,1,0:T(8,128)(2,1)S(1)}, bf16[5,2,96,128]{3,2,1,0:T(8,128)(2,1)S(1)}, u32[]{:S(2)}, u32[]{:S(2)}) collective-permute-start(bf16[5,2,96,128]{3,2,1,0:T(8,128)(2,1)S(1)} %bitcast.22), channel_id=1, source_target_pairs={{0,8},{8,0},{16,24},{24,16},{32,40},{40,32},{48,56},{56,48},{64,72... | collective-permute-start | bytes 737288 | tf_op jit(solution)/shard_map/ppermute | solution.py:234
  8.1 0.7 copy.16
  8.8 0.7 convert_element_type.11
  9.5 0.8 copy.18.cb_ref
  10.3 1.4 %copy.17.wt_ref = bf16[96,2592]{1,0:T(8,128)(2,1)S(1)} copy(bf16[96,2592]{0,1:T(8,128)(2,1)} %bitcast.27) | data formatting | bytes 995328 | tf_op jit(solution)/shard_map/reshape | solution.py:236
  11.7 0.0 copy-done.1
  11.7 0.7 collective-permute-done.1
  12.5 1.8 %collective-permute-done = bf16[5,2,96,128]{3,2,1,0:T(8,128)(2,1)S(1)} collective-permute-done((bf16[5,2,96,128]{3,2,1,0:T(8,128)(2,1)S(1)}, bf16[5,2,96,128]{3,2,1,0:T(8,128)(2,1)S(1)}, u32[]{:S(2)}, u32[]{:S(2)}) %collective-permute-start) | collective-permute-done | bytes 245792 | tf_op jit(solution)/shard_map/ppermute | solution.py:234
  14.3 7.1 %device_part.1 = (f32[8,1280]{1,0:T(8,128)S(1)}, bf16[2048,128]{1,0:T(8,128)(2,1)S(1)}) custom-call(bf16[5,2,96,128]{3,2,1,0:T(8,128)(2,1)S(1)} %bitcast.23, bf16[2,5,2,96,128]{4,3,2,1,0:T(8,128)(2,1)S(1)} %pad_maximum_fusion.pair_ref, bf16[96,2592]{1,0:T(8,128)(2,1)S(1)} %copy.17.wt_ref, f32[96,1]{1,0:T(8,128)S(1)} %copy.18.cb_ref, ...), custom_call_target="tpu_custom_call" | custom-call | tf_op jit(solution)/shard_map/device_part/pallas_call | solution.py:241
  21.4 19.3 %all_to_all.15.in_ref = bf16[32,64,128]{2,1,0:T(8,128)(2,1)} all-to-all(bf16[32,64,128]{2,1,0:T(8,128)(2,1)S(1)} %bitcast.24), channel_id=1, replica_groups=mesh['x'=4,'zl'=4,'y'=4,'zh'=4,'c'=2] {'x','y','c'}, dimensions={0} | all-to-all | bytes 1048576 | tf_op jit(solution)/shard_map/all_to_all | solution.py:275
  40.7 1.9 %sum_parts.2 = bf16[16,64,128]{2,1,0:T(8,128)(2,1)} custom-call(bf16[32,64,128]{2,1,0:T(8,128)(2,1)} %all_to_all.15.in_ref), custom_call_target="tpu_custom_call" | custom-call | tf_op jit(solution)/shard_map/sum_parts/pallas_call | solution.py:267
  42.6 32.9 %all_to_all.16.in_ref = bf16[16,64,128]{2,1,0:T(8,128)(2,1)} all-to-all(bf16[16,64,128]{2,1,0:T(8,128)(2,1)} %sum_parts.2), channel_id=1, replica_groups=mesh['x'=4,'zl'=4,'y'=4,'zh'=4,'c'=2] {'zl','zh'}, dimensions={0} | all-to-all | bytes 524288 | tf_op jit(solution)/shard_map/all_to_all | solution.py:276
  75.5 1.9 %sum_parts.3 = bf16[32,64,128]{2,1,0:T(8,128)(2,1)} custom-call(bf16[16,64,128]{2,1,0:T(8,128)(2,1)} %all_to_all.16.in_ref), custom_call_target="tpu_custom_call" | custom-call | tf_op jit(solution)/shard_map/sum_parts/pallas_call | solution.py:267
  77.3 6.7 %all-to-all-start.2 = ((bf16[32,64,128]{2,1,0:T(8,128)(2,1)}), bf16[32,64,128]{2,1,0:T(8,128)(2,1)S(1)}, u32[]{:S(2)}, u32[]{:S(2)}) async-start(bf16[32,64,128]{2,1,0:T(8,128)(2,1)} %sum_parts.3), calls=%async_computation.2 | async-start | bytes 1048576 | tf_op jit(solution)/shard_map/all_to_all | solution.py:277
  84.1 0.6 reshape.35
  84.7 11.1 %all-to-all-done.2 = bf16[32,64,128]{2,1,0:T(8,128)(2,1)S(1)} async-done(((bf16[32,64,128]{2,1,0:T(8,128)(2,1)}), bf16[32,64,128]{2,1,0:T(8,128)(2,1)S(1)}, u32[]{:S(2)}, u32[]{:S(2)}) %all-to-all-start.2) | async-done | bytes 524320 | tf_op jit(solution)/shard_map/all_to_all | solution.py:277
  95.8 0.0 copy-start
  95.8 0.8 copy-done
  96.6 2.4 %unpack.1 = (f32[2592,96]{1,0:T(8,128)}, f32[1,96]{1,0:T(1,128)}, f32[3,27,96]{2,1,0:T(8,128)}, f32[1,128]{1,0:T(1,128)}) custom-call(bf16[2048,128]{1,0:T(8,128)(2,1)} %bitcast.26), custom_call_target="tpu_custom_call" | custom-call | tf_op jit(solution)/shard_map/unpack/pallas_call | solution.py:279
  98.9 1.1 %slice_bitcast_fusion = f32[3]{0:T(128)} fusion(f32[1,128]{1,0:T(1,128)} %get-tuple-element.16), kind=kLoop, calls=%fused_computation.4 | loop fusion | bytes 24 | tf_op jit(solution)/shard_map/squeeze | solution.py:297
  (5 shorter events, 0.1 us)
Async XLA Ops:
  0.6 11.1 %copy-start.1 = (bf16[27,96,3]{1,0,2:T(8,128)(2,1)S(1)}, bf16[27,96,3]{1,0,2:T(8,128)(2,1)}, u32[]{:S(2)}) copy-start(bf16[27,96,3]{1,0,2:T(8,128)(2,1)} %param.9) | copy-start | bytes 46660
  1.6 10.8 %collective-permute-start.1 = (bf16[5,2,96,128]{3,2,1,0:T(8,128)(2,1)S(1)}, bf16[5,2,96,128]{3,2,1,0:T(8,128)(2,1)S(1)}, u32[]{:S(2)}, u32[]{:S(2)}) collective-permute-start(bf16[5,2,96,128]{3,2,1,0:T(8,128)(2,1)S(1)} %bitcast.21), channel_id=1, source_target_pairs={{8,16},{16,8},{24,32},{32,24},{40,48},{48,40},{56,64},{64,56},{72,... | collective-permute-start | bytes 737288 | tf_op jit(solution)/shard_map/ppermute | solution.py:234
  5.8 8.4 %collective-permute-start = (bf16[5,2,96,128]{3,2,1,0:T(8,128)(2,1)S(1)}, bf16[5,2,96,128]{3,2,1,0:T(8,128)(2,1)S(1)}, u32[]{:S(2)}, u32[]{:S(2)}) collective-permute-start(bf16[5,2,96,128]{3,2,1,0:T(8,128)(2,1)S(1)} %bitcast.22), channel_id=1, source_target_pairs={{0,8},{8,0},{16,24},{24,16},{32,40},{40,32},{48,56},{56,48},{64,72... | collective-permute-start | bytes 737288 | tf_op jit(solution)/shard_map/ppermute | solution.py:234
  77.3 18.5 %all-to-all-start.2 = ((bf16[32,64,128]{2,1,0:T(8,128)(2,1)}), bf16[32,64,128]{2,1,0:T(8,128)(2,1)S(1)}, u32[]{:S(2)}, u32[]{:S(2)}) async-start(bf16[32,64,128]{2,1,0:T(8,128)(2,1)} %sum_parts.3), calls=%async_computation.2 | async-start | bytes 1048576 | tf_op jit(solution)/shard_map/all_to_all | solution.py:277
  95.8 0.8 copy-start

commit v2 on v1

v2 whole, which is shorter than its diff:
```python
import functools
import math

import jax
import jax.numpy as jnp
from jax import lax
from jax.experimental import pallas as pl
from jax.experimental.pallas import tpu as pltpu
from jax.sharding import Mesh, PartitionSpec as P

BF = jnp.bfloat16
F32 = jnp.float32
C = 96
F = 5
W = 128
TAPS = 27
TPAD = 28
OPAD = 8
GROWS = TPAD * OPAD
HR = 4
FW = HR * W
POS = F * FW
KT = 9 * C
NW = TAPS * C
MAIN = 1920
TAIL = NW - MAIN
ROWS = 2048
EDGE_AXES = ("x", "z1", "z0", "y")
NEAR = ("x", "z0", "y", "c")
DEPTH = ("z1", "zh")


def nt(a, b):
    return lax.dot_general(a, b, (((1,), (1,)), ((), ())), preferred_element_type=F32)


def nn(a, b):
    return lax.dot_general(a, b, (((1,), (0,)), ((), ())), preferred_element_type=F32)


def tn(a, b):
    return lax.dot_general(a, b, (((0,), (0,)), ((), ())), preferred_element_type=F32)


def shifted(v, lane, by):
    if by == 0:
        return v
    if by > 0:
        return jnp.where(lane < W - 1, pltpu.roll(v, W - 1, 1), 0.0)
    return jnp.where(lane > 0, pltpu.roll(v, 1, 1), 0.0)


def flat_index(axes):
    index = 0
    for axis in axes:
        index = index * lax.axis_size(axis) + lax.axis_index(axis)
    return index


def device_kernel(
    n_rows, scale,
    own_ref, pair_ref, wt_ref, cb_ref, wo_ref, ob_ref, tgt_ref,
    dec_ref, pay_ref,
    q_ref, r_ref, hid_ref, fac_ref, y_ref, g_ref, gh_ref, main_ref,
):
    row_id = flat_index(EDGE_AXES)
    odd = lax.rem(row_id, 2)
    first = row_id == 0
    last = row_id == n_rows - 1
    lane96 = lax.broadcasted_iota(jnp.int32, (C, W), 1)
    lane8 = lax.broadcasted_iota(jnp.int32, (OPAD, W), 1)

    for g in range(F):
        for r in range(6):
            if r < 2:
                tile = pair_ref[1 - odd, g, r]
            elif r < 4:
                tile = own_ref[g, r - 2]
            else:
                tile = pair_ref[odd, g, r - 4]
            wide = tile.astype(F32)
            for kj in range(3):
                piece = tile if kj == 1 else shifted(wide, lane96, kj - 1).astype(BF)
                for ki in range(3):
                    i = r - ki
                    if 0 <= i < HR:
                        base = (ki * 3 + kj) * C
                        q_ref[base : base + C, g * FW + i * W : g * FW + (i + 1) * W] = piece

    srow = lax.broadcasted_iota(jnp.int32, (C, GROWS), 0)
    scol = lax.broadcasted_iota(jnp.int32, (C, GROWS), 1)
    pick = ((srow // 32 == scol % OPAD) & (srow % 32 == scol // OPAD)).astype(F32).astype(BF)
    wo = wo_ref[...]
    wo8 = tn(pick, wo).astype(BF)
    wo8t = tn(wo, pick).astype(BF)

    col = lax.broadcasted_iota(jnp.int32, (1, FW), 1)
    outside = ((col < W) & first) | ((col >= 3 * W) & last)
    keep = jnp.where(outside, 0.0, 1.0)
    for f in range(F):
        low = max(0, f - 2) * C
        r_ref[f, low:, :] = nn(wt_ref[low:, :], q_ref[:, f * FW : (f + 1) * FW])
        pre = cb_ref[...]
        for kt in range(2, max(-1, 1 - f), -1):
            pre = pre + r_ref[f + kt - 2, kt * C : (kt + 1) * C, :]
        sig = jax.nn.sigmoid(pre)
        hid = (pre * sig * keep).astype(BF)
        hid_ref[:, f * FW : (f + 1) * FW] = hid
        fac_ref[:, f * FW : (f + 1) * FW] = sig * (1.0 + pre * (1.0 - sig)) * keep
        y_ref[:, f * FW : (f + 1) * FW] = nn(wo8, hid)

    grads = {}
    obsum = jnp.zeros((OPAD, W), F32)
    for f in range(F):
        decs = []
        for i in range(2):
            dec = None
            for kj in range(3):
                z = None
                for kt in range(3):
                    g = f + kt - 2
                    if g < 0:
                        continue
                    for ki in range(3):
                        t = kt * 9 + ki * 3 + kj
                        at = g * FW + (i + ki) * W
                        v = y_ref[t * OPAD : (t + 1) * OPAD, at : at + W]
                        z = v if z is None else z + v
                z = shifted(z, lane8, kj - 1)
                dec = z if dec is None else dec + z
            dec = (dec + ob_ref[...]).astype(BF)
            at = (f * 2 + i) * W
            decs.append(dec.astype(F32))
            gf = ((dec.astype(F32) - tgt_ref[:, at : at + W]) * scale).astype(BF).astype(F32)
            obsum = obsum + gf
            for kj in range(3):
                grads[f, i, kj] = shifted(gf, lane8, 1 - kj)
        for o in range(3):
            rows = jnp.concatenate([d[o : o + 1] for d in decs], axis=0)
            dec_ref[0, o, f] = rows.astype(BF)

    none = jnp.zeros((OPAD, W), F32)
    for g in range(F):
        for i in range(HR):
            parts = []
            for t in range(TPAD):
                kt, ki, kj = t // 9, t // 3 % 3, t % 3
                parts.append(grads.get((g + 2 - kt, i - ki, kj), none) if t < TAPS else none)
            at = g * FW + i * W
            for p in range(TPAD // 2):
                both = jnp.concatenate(parts[2 * p : 2 * p + 2], axis=0).astype(BF)
                g_ref[p * 16 : (p + 1) * 16, at : at + W] = both

    gh_ref[C:W, :] = jnp.zeros((W - C, POS), BF)
    gh_ref[W + C :, :] = jnp.zeros((W - C, POS), BF)
    gh_ref[W:, POS - FW :] = jnp.zeros((W, FW), BF)
    for f in range(F):
        back = nn(wo8t, g_ref[:, f * FW : (f + 1) * FW])
        gh = (back * fac_ref[:, f * FW : (f + 1) * FW]).astype(BF)
        gh_ref[:C, f * FW : (f + 1) * FW] = gh
        if f:
            gh_ref[W : W + C, (f - 1) * FW : f * FW] = gh

    both = nt(q_ref[...], gh_ref[...])
    main_ref[2 * KT :, :] = both[:, :W]
    main_ref[KT : 2 * KT, :] = both[:, W:]
    main_ref[:KT, :] = nt(q_ref[:, : 3 * FW], gh_ref[:W, 2 * FW :])
    gow = nt(g_ref[...], hid_ref[...]).astype(BF)
    gow = nn(pick, gow)
    bias = nt(jnp.ones((OPAD, POS), BF), gh_ref[:W, :])
    obias = jnp.broadcast_to(jnp.sum(obsum, axis=1, keepdims=True), (OPAD, W))

    lane = lax.broadcasted_iota(jnp.int32, (TAIL, W), 1)
    for k in range(3):
        lo, hi = k * TAIL, (k + 1) * TAIL
        tail = pltpu.roll(main_ref[MAIN:, :], 96 - 32 * k, 1)
        if hi <= MAIN:
            head = main_ref[lo:hi, :]
        else:
            head = jnp.concatenate(
                [main_ref[lo:MAIN, :], jnp.pad(gow, ((0, 0), (0, W - C)))], axis=0
            )
        pay_ref[lo:hi, :] = jnp.where(lane < C, head, tail).astype(BF)
    for at, v in ((2016, bias), (2032, obias)):
        top = v.astype(BF).astype(F32)
        pay_ref[at : at + 16, :] = jnp.concatenate([top, v - top], axis=0).astype(BF)


def split_sums(total, is_last):
    out = total.astype(BF)
    start = total.shape[0] - 32
    fixed = []
    for at in (start, start + 16):
        whole = total[at : at + 8] + total[at + 8 : at + 16]
        top = whole.astype(BF).astype(F32)
        fixed += [top, whole - top]
    special = jnp.concatenate(([total[:start]] if start else []) + fixed, axis=0).astype(BF)
    return jnp.where(is_last, special, out)


def sum_kernel(in_ref, out_ref):
    total = in_ref[0].astype(F32)
    for k in range(1, in_ref.shape[0]):
        total = total + in_ref[k].astype(F32)
    count = math.prod(lax.axis_size(a) for a in NEAR)
    res = split_sums(total, flat_index(NEAR) == count - 1)
    for k in range(out_ref.shape[0]):
        out_ref[k] = res


def unpack_kernel(in_ref, gw_ref, gb_ref, go_ref, gob_ref):
    def get(lo, hi):
        return in_ref[lo:hi, :].astype(F32)

    gw_ref[:MAIN, :] = get(0, MAIN)[:, :C]
    lane = lax.broadcasted_iota(jnp.int32, (TAIL, W), 1)
    tail = None
    for k in range(3):
        v = pltpu.roll(get(k * TAIL, (k + 1) * TAIL), 32 + 32 * k, 1)
        tail = v if tail is None else jnp.where(lane < 32 * k, tail, v)
    gw_ref[MAIN:, :] = tail[:, :C]
    gow = get(MAIN, MAIN + 96)
    for o in range(3):
        go_ref[o] = gow[o * 32 : o * 32 + TAPS, :C]
    sums = get(2016, 2048)
    gb_ref[...] = (sums[0:8] + sums[8:16])[0, :C]
    ob = sums[16:24] + sums[24:32]
    r8 = lax.broadcasted_iota(jnp.int32, (OPAD, W), 0)
    l8 = lax.broadcasted_iota(jnp.int32, (OPAD, W), 1)
    gob_ref[...] = jnp.sum(jnp.where(r8 == l8, ob, 0.0), axis=0)[:3]


VM = functools.partial(pl.BlockSpec, memory_space=pltpu.VMEM)
LIMIT = 48 * 1024 * 1024
SMALL = 4 * 1024 * 1024


def k1_call(n_rows, scale):
    return pl.pallas_call(
        functools.partial(device_kernel, n_rows, scale),
        out_shape=(
            jax.ShapeDtypeStruct((1, 3, F, 2, W), BF),
            jax.ShapeDtypeStruct((ROWS, W), BF),
        ),
        in_specs=[VM()] * 7,
        out_specs=(VM(), VM()),
        scratch_shapes=[
            pltpu.VMEM((KT, POS), BF),
            pltpu.VMEM((F, 3 * C, FW), F32),
            pltpu.VMEM((C, POS), BF),
            pltpu.VMEM((C, POS), F32),
            pltpu.VMEM((GROWS, POS), F32),
            pltpu.VMEM((GROWS, POS), BF),
            pltpu.VMEM((2 * W, POS), BF),
            pltpu.VMEM((NW, W), F32),
        ],
        compiler_params=pltpu.CompilerParams(vmem_limit_bytes=LIMIT),
        name="device_part",
    )


def local(latent_features, conv_weight, conv_bias, out_weight, out_bias, target_frames):
    sizes = [lax.axis_size(a) for a in EDGE_AXES]
    n_rows = math.prod(sizes)
    clips = lax.axis_size("zh") * lax.axis_size("c")
    scale = 1.0 / math.sqrt(3 * clips * F * 2 * n_rows * W)

    own = jnp.transpose(latent_features[0], (1, 2, 0, 3))
    even = [(i, i ^ 1) for i in range(n_rows)]
    odd = [(i, ((i + 1) ^ 1) - 1) for i in range(1, n_rows - 1)]
    pair = jnp.stack([lax.ppermute(own, EDGE_AXES, even), lax.ppermute(own, EDGE_AXES, odd)])

    wt = jnp.transpose(conv_weight.reshape(3, KT, C), (0, 2, 1)).reshape(3 * C, KT)
    wo = jnp.pad(jnp.transpose(out_weight, (2, 0, 1)), ((0, 0), (0, 5), (0, 0))).reshape(C, C)
    ob = jnp.pad(out_bias[:, None], ((0, 5), (0, 0)))
    tgt = jnp.pad(target_frames[0].reshape(3, F * 2 * W).astype(F32), ((0, 5), (0, 0)))

    decoded, packed = k1_call(n_rows, scale)(own, pair, wt, conv_bias[:, None], wo, ob, tgt)

    near = math.prod(lax.axis_size(a) for a in NEAR)
    depth = math.prod(lax.axis_size(a) for a in DEPTH)
    chunk = ROWS // near

    def summed(parts, copies):
        return pl.pallas_call(
            sum_kernel,
            out_shape=jax.ShapeDtypeStruct((copies, chunk, W), BF),
            in_specs=[VM()],
            out_specs=VM(),
            compiler_params=pltpu.CompilerParams(vmem_limit_bytes=SMALL),
            name="sum_parts",
        )(parts)

    parts = lax.all_to_all(packed.reshape(near, chunk, W), NEAR, 0, 0)
    parts = lax.all_to_all(summed(parts, depth), DEPTH, 0, 0)
    parts = lax.all_to_all(summed(parts, near), NEAR, 0, 0)

    gw, gb, go, gob = pl.pallas_call(
        unpack_kernel,
        out_shape=(
            jax.ShapeDtypeStruct((NW, C), F32),
            jax.ShapeDtypeStruct((C,), F32),
            jax.ShapeDtypeStruct((3, TAPS, C), F32),
            jax.ShapeDtypeStruct((3,), F32),
        ),
        in_specs=[VM()],
        out_specs=(VM(),) * 4,
        compiler_params=pltpu.CompilerParams(vmem_limit_bytes=2 * SMALL),
        name="unpack",
    )(parts.reshape(ROWS, W))
    return (
        decoded,
        gw.reshape(TAPS, C, C),
        gb,
        jnp.transpose(go, (1, 2, 0)),
        gob,
    )


def solution(mesh):
    split = Mesh(mesh.devices.reshape(4, 2, 2, 4, 4, 2), ("x", "z1", "z0", "y", "zh", "c"))
    frames = P(("zh", "c"), None, None, EDGE_AXES, None)
    return jax.shard_map(
        local,
        mesh=split,
        in_specs=(frames, P(), P(), P(), P(), frames),
        out_specs=(frames, P(), P(), P(), P()),
        check_vma=False,
    )
```

time: 101 us -> 89.2 us (0.88)
  the two profiles are of different devices: /device:TPU:33 before, /device:TPU:1 now
where the time goes in v2:
time: 89.2 us; the launch traced here: 88.8 us
  blocking collectives  69.1 us (77%)
  starting transfers between devices  7.24 us (8%)
  Pallas kernels  7.14 us (8%)
  local copies, waits for them, and re-layouts  4.62 us (5%)
    all_to_all x1, blocking collectives, local(): parts = lax.all_to_all(packed.reshape(near, chunk, W), NEAR, 0, 0)  25.9 us
    all_to_all x1, blocking collectives, local(): parts = lax.all_to_all(summed(parts, depth), DEPTH, 0, 0)  24.3 us
    all_to_all x1, blocking collectives, local(): parts = lax.all_to_all(summed(parts, near), NEAR, 0, 0)  18.8 us
    ppermute x1, starting transfers between devices, local(): lax.ppermute(own, EDGE_AXES, even)  6.56 us
    pallas_call x1, Pallas kernels, local(): k1_call(n_rows, scale)(own, pair, wt, conv_bias[:, None], wo, ob, tgt)  5.63 us
  transfers between devices with their start and end apart: 2, of which 0 were waited for; matrix products, arithmetic and copies ran while one was open for 4% of the time, Pallas kernels for 0%

profile of v2, /device:TPU:1, one launch (start us, length us, event | category | flops | bytes accessed | tf_op | source)
XLA Modules:
  0.0 88.8 jit_solution(525675012029640550)
XLA Ops:
  0.6 0.0 copy-start
  0.6 1.0 %copy.16 = bf16[1,96,5,2,128]{4,1,3,2,0:T(8,128)(2,1)S(1)} copy(bf16[1,96,5,2,128]{4,3,2,1,0:T(2,128)(2,1)} %param.6) | data formatting | bytes 491520 | tf_op args[0]
  1.6 0.7 collective-permute-start.1
  2.3 6.6 %collective-permute-start = (bf16[5,2,96,128]{3,2,1,0:T(8,128)(2,1)S(1)}, bf16[5,2,96,128]{3,2,1,0:T(8,128)(2,1)S(1)}, u32[]{:S(2)}, u32[]{:S(2)}) collective-permute-start(bf16[5,2,96,128]{3,2,1,0:T(8,128)(2,1)S(1)} %bitcast.22), channel_id=1, source_target_pairs={{0,8},{8,0},{16,24},{24,16},{32,40},{40,32},{48,56},{56,48},{64,72... | collective-permute-start | bytes 737288 | tf_op jit(solution)/shard_map/ppermute | solution.py:271
  8.9 0.7 copy.13
  9.6 0.7 convert_element_type.10
  10.3 0.8 copy.14.cb_ref
  11.1 1.4 %copy.12 = bf16[3,864,96]{1,2,0:T(8,128)(2,1)S(1)} copy(bf16[3,864,96]{2,1,0:T(8,128)(2,1)} %bitcast.26) | data formatting | bytes 995328 | tf_op jit(solution)/shard_map/reshape | solution.py:273
  12.5 0.0 copy-done
  12.6 0.0 collective-permute-done.1
  12.6 0.0 collective-permute-done
  12.6 5.6 %device_part.1 = (bf16[1,3,5,2,128]{4,3,2,1,0:T(2,128)(2,1)}, bf16[2048,128]{1,0:T(8,128)(2,1)S(1)}) custom-call(bf16[5,2,96,128]{3,2,1,0:T(8,128)(2,1)S(1)} %bitcast.23, bf16[2,5,2,96,128]{4,3,2,1,0:T(8,128)(2,1)S(1)} %pad_maximum_fusion.pair_ref, bf16[288,864]{1,0:T(8,128)(2,1)S(1)} %bitcast.20, f32[96,1]{1,0:T(8,128)S(1)} %copy.14.cb_ref, ...), custom_call_target="tpu_custom_call" | custom-call | tf_op jit(solution)/shard_map/device_part/pallas_call | solution.py:278
  18.3 25.9 %all_to_all.15.in_ref = bf16[64,32,128]{2,1,0:T(8,128)(2,1)S(1)} all-to-all(bf16[64,32,128]{2,1,0:T(8,128)(2,1)S(1)} %bitcast.24), channel_id=1, replica_groups=mesh['x'=4,'z1'=2,'z0'=2,'y'=4,'zh'=4,'c'=2] {'x','z0','y','c'}, dimensions={0} | all-to-all | bytes 1048576 | tf_op jit(solution)/shard_map/all_to_all | solution.py:294
  44.2 0.1 sum_parts.2
  44.3 24.3 %all_to_all.16.in_ref = bf16[8,32,128]{2,1,0:T(8,128)(2,1)S(1)} all-to-all(bf16[8,32,128]{2,1,0:T(8,128)(2,1)S(1)} %sum_parts.2), channel_id=1, replica_groups=mesh['x'=4,'z1'=2,'z0'=2,'y'=4,'zh'=4,'c'=2] {'z1','zh'}, dimensions={0} | all-to-all | bytes 131072 | tf_op jit(solution)/shard_map/all_to_all | solution.py:295
  68.6 0.1 sum_parts.3
  68.7 18.8 %all_to_all.17 = bf16[64,32,128]{2,1,0:T(8,128)(2,1)S(1)} all-to-all(bf16[64,32,128]{2,1,0:T(8,128)(2,1)S(1)} %sum_parts.3), channel_id=1, replica_groups=mesh['x'=4,'z1'=2,'z0'=2,'y'=4,'zh'=4,'c'=2] {'x','z0','y','c'}, dimensions={0} | all-to-all | bytes 1048576 | tf_op jit(solution)/shard_map/all_to_all | solution.py:296
  87.5 1.3 %unpack.1 = (f32[2592,96]{1,0:T(8,128)}, f32[96]{0:T(128)}, f32[3,27,96]{2,1,0:T(8,128)}, f32[3]{0:T(128)}) custom-call(bf16[2048,128]{1,0:T(8,128)(2,1)S(1)} %bitcast.19), custom_call_target="tpu_custom_call" | custom-call | tf_op jit(solution)/shard_map/unpack/pallas_call | solution.py:298
  (4 shorter events, 0.1 us)
Async XLA Ops:
  0.6 11.9 %copy-start = (bf16[27,96,3]{1,0,2:T(8,128)(2,1)S(1)}, bf16[27,96,3]{1,0,2:T(8,128)(2,1)}, u32[]{:S(2)}) copy-start(bf16[27,96,3]{1,0,2:T(8,128)(2,1)} %param.9) | copy-start | bytes 46660
  1.6 10.9 %collective-permute-start.1 = (bf16[5,2,96,128]{3,2,1,0:T(8,128)(2,1)S(1)}, bf16[5,2,96,128]{3,2,1,0:T(8,128)(2,1)S(1)}, u32[]{:S(2)}, u32[]{:S(2)}) collective-permute-start(bf16[5,2,96,128]{3,2,1,0:T(8,128)(2,1)S(1)} %bitcast.21), channel_id=1, source_target_pairs={{8,16},{16,8},{24,32},{32,24},{40,48},{48,40},{56,64},{64,56},{72,... | collective-permute-start | bytes 737288 | tf_op jit(solution)/shard_map/ppermute | solution.py:271
  2.3 10.3 %collective-permute-start = (bf16[5,2,96,128]{3,2,1,0:T(8,128)(2,1)S(1)}, bf16[5,2,96,128]{3,2,1,0:T(8,128)(2,1)S(1)}, u32[]{:S(2)}, u32[]{:S(2)}) collective-permute-start(bf16[5,2,96,128]{3,2,1,0:T(8,128)(2,1)S(1)} %bitcast.22), channel_id=1, source_target_pairs={{0,8},{8,0},{16,24},{24,16},{32,40},{40,32},{48,56},{56,48},{64,72... | collective-permute-start | bytes 737288 | tf_op jit(solution)/shard_map/ppermute | solution.py:271

commit v3 on v2

--- a/solution.py
+++ b/solution.py
@@ -97,17 +97,28 @@
     col = lax.broadcasted_iota(jnp.int32, (1, FW), 1)
     outside = ((col < W) & first) | ((col >= 3 * W) & last)
     keep = jnp.where(outside, 0.0, 1.0)
-    for f in range(F):
+    def conv(f):
         low = max(0, f - 2) * C
         r_ref[f, low:, :] = nn(wt_ref[low:, :], q_ref[:, f * FW : (f + 1) * FW])
+
+    def activate(f):
         pre = cb_ref[...]
         for kt in range(2, max(-1, 1 - f), -1):
             pre = pre + r_ref[f + kt - 2, kt * C : (kt + 1) * C, :]
         sig = jax.nn.sigmoid(pre)
-        hid = (pre * sig * keep).astype(BF)
-        hid_ref[:, f * FW : (f + 1) * FW] = hid
+        hid_ref[:, f * FW : (f + 1) * FW] = (pre * sig * keep).astype(BF)
         fac_ref[:, f * FW : (f + 1) * FW] = sig * (1.0 + pre * (1.0 - sig)) * keep
-        y_ref[:, f * FW : (f + 1) * FW] = nn(wo8, hid)
+
+    def project(f):
+        y_ref[:, f * FW : (f + 1) * FW] = nn(wo8, hid_ref[:, f * FW : (f + 1) * FW])
+
+    for f in range(F + 2):
+        if f < F:
+            conv(f)
+        if 1 <= f <= F:
+            activate(f - 1)
+        if f >= 2:
+            project(f - 2)
 
     grads = {}
     obsum = jnp.zeros((OPAD, W), F32)

time: 89.2 us -> 88.5 us (level)
  no operation moved by 1% of the time
where the time goes in v3:
time: 88.5 us; the launch traced here: 88.2 us
  blocking collectives  69.1 us (78%)
  starting transfers between devices  7.24 us (8%)
  Pallas kernels  6.46 us (7%)
  local copies, waits for them, and re-layouts  4.62 us (5%)
    all_to_all x1, blocking collectives, local(): parts = lax.all_to_all(packed.reshape(near, chunk, W), NEAR, 0, 0)  25.9 us
    all_to_all x1, blocking collectives, local(): parts = lax.all_to_all(summed(parts, depth), DEPTH, 0, 0)  24.3 us
    all_to_all x1, blocking collectives, local(): parts = lax.all_to_all(summed(parts, near), NEAR, 0, 0)  18.8 us
    ppermute x1, starting transfers between devices, local(): lax.ppermute(own, EDGE_AXES, even)  6.56 us
    pallas_call x1, Pallas kernels, local(): k1_call(n_rows, scale)(own, pair, wt, conv_bias[:, None], wo, ob, tgt)  4.96 us
  transfers between devices with their start and end apart: 2, of which 0 were waited for; matrix products, arithmetic and copies ran while one was open for 4% of the time, Pallas kernels for 0%

profile of v3, /device:TPU:1, one launch (start us, length us, event | category | flops | bytes accessed | tf_op | source)
XLA Modules:
  0.0 88.2 jit_solution(13546308077697902173)
XLA Ops:
  0.6 0.0 copy-start
  0.6 1.0 %copy.16 = bf16[1,96,5,2,128]{4,1,3,2,0:T(8,128)(2,1)S(1)} copy(bf16[1,96,5,2,128]{4,3,2,1,0:T(2,128)(2,1)} %param.6) | data formatting | bytes 491520 | tf_op args[0]
  1.6 0.7 collective-permute-start.1
  2.3 6.6 %collective-permute-start = (bf16[5,2,96,128]{3,2,1,0:T(8,128)(2,1)S(1)}, bf16[5,2,96,128]{3,2,1,0:T(8,128)(2,1)S(1)}, u32[]{:S(2)}, u32[]{:S(2)}) collective-permute-start(bf16[5,2,96,128]{3,2,1,0:T(8,128)(2,1)S(1)} %bitcast.22), channel_id=1, source_target_pairs={{0,8},{8,0},{16,24},{24,16},{32,40},{40,32},{48,56},{56,48},{64,72... | collective-permute-start | bytes 737288 | tf_op jit(solution)/shard_map/ppermute | solution.py:282
  8.9 0.7 copy.13
  9.6 0.7 convert_element_type.10
  10.3 0.8 copy.14.cb_ref
  11.1 1.4 %copy.12 = bf16[3,864,96]{1,2,0:T(8,128)(2,1)S(1)} copy(bf16[3,864,96]{2,1,0:T(8,128)(2,1)} %bitcast.26) | data formatting | bytes 995328 | tf_op jit(solution)/shard_map/reshape | solution.py:284
  12.5 0.0 copy-done
  12.6 0.0 collective-permute-done.1
  12.6 0.0 collective-permute-done
  12.6 5.0 %device_part.1 = (bf16[1,3,5,2,128]{4,3,2,1,0:T(2,128)(2,1)}, bf16[2048,128]{1,0:T(8,128)(2,1)S(1)}) custom-call(bf16[5,2,96,128]{3,2,1,0:T(8,128)(2,1)S(1)} %bitcast.23, bf16[2,5,2,96,128]{4,3,2,1,0:T(8,128)(2,1)S(1)} %pad_maximum_fusion.pair_ref, bf16[288,864]{1,0:T(8,128)(2,1)S(1)} %bitcast.20, f32[96,1]{1,0:T(8,128)S(1)} %copy.14.cb_ref, ...), custom_call_target="tpu_custom_call" | custom-call | tf_op jit(solution)/shard_map/device_part/pallas_call | solution.py:289
  17.6 25.9 %all_to_all.15.in_ref = bf16[64,32,128]{2,1,0:T(8,128)(2,1)S(1)} all-to-all(bf16[64,32,128]{2,1,0:T(8,128)(2,1)S(1)} %bitcast.24), channel_id=1, replica_groups=mesh['x'=4,'z1'=2,'z0'=2,'y'=4,'zh'=4,'c'=2] {'x','z0','y','c'}, dimensions={0} | all-to-all | bytes 1048576 | tf_op jit(solution)/shard_map/all_to_all | solution.py:305
  43.5 0.1 sum_parts.2
  43.6 24.3 %all_to_all.16.in_ref = bf16[8,32,128]{2,1,0:T(8,128)(2,1)S(1)} all-to-all(bf16[8,32,128]{2,1,0:T(8,128)(2,1)S(1)} %sum_parts.2), channel_id=1, replica_groups=mesh['x'=4,'z1'=2,'z0'=2,'y'=4,'zh'=4,'c'=2] {'z1','zh'}, dimensions={0} | all-to-all | bytes 131072 | tf_op jit(solution)/shard_map/all_to_all | solution.py:306
  67.9 0.1 sum_parts.3
  68.0 18.8 %all_to_all.17 = bf16[64,32,128]{2,1,0:T(8,128)(2,1)S(1)} all-to-all(bf16[64,32,128]{2,1,0:T(8,128)(2,1)S(1)} %sum_parts.3), channel_id=1, replica_groups=mesh['x'=4,'z1'=2,'z0'=2,'y'=4,'zh'=4,'c'=2] {'x','z0','y','c'}, dimensions={0} | all-to-all | bytes 1048576 | tf_op jit(solution)/shard_map/all_to_all | solution.py:307
  86.8 1.3 %unpack.1 = (f32[2592,96]{1,0:T(8,128)}, f32[96]{0:T(128)}, f32[3,27,96]{2,1,0:T(8,128)}, f32[3]{0:T(128)}) custom-call(bf16[2048,128]{1,0:T(8,128)(2,1)S(1)} %bitcast.19), custom_call_target="tpu_custom_call" | custom-call | tf_op jit(solution)/shard_map/unpack/pallas_call | solution.py:309
  (4 shorter events, 0.1 us)
Async XLA Ops:
  0.6 11.9 %copy-start = (bf16[27,96,3]{1,0,2:T(8,128)(2,1)S(1)}, bf16[27,96,3]{1,0,2:T(8,128)(2,1)}, u32[]{:S(2)}) copy-start(bf16[27,96,3]{1,0,2:T(8,128)(2,1)} %param.9) | copy-start | bytes 46660
  1.6 10.9 %collective-permute-start.1 = (bf16[5,2,96,128]{3,2,1,0:T(8,128)(2,1)S(1)}, bf16[5,2,96,128]{3,2,1,0:T(8,128)(2,1)S(1)}, u32[]{:S(2)}, u32[]{:S(2)}) collective-permute-start(bf16[5,2,96,128]{3,2,1,0:T(8,128)(2,1)S(1)} %bitcast.21), channel_id=1, source_target_pairs={{8,16},{16,8},{24,32},{32,24},{40,48},{48,40},{56,64},{64,56},{72,... | collective-permute-start | bytes 737288 | tf_op jit(solution)/shard_map/ppermute | solution.py:282
  2.3 10.3 %collective-permute-start = (bf16[5,2,96,128]{3,2,1,0:T(8,128)(2,1)S(1)}, bf16[5,2,96,128]{3,2,1,0:T(8,128)(2,1)S(1)}, u32[]{:S(2)}, u32[]{:S(2)}) collective-permute-start(bf16[5,2,96,128]{3,2,1,0:T(8,128)(2,1)S(1)} %bitcast.22), channel_id=1, source_target_pairs={{0,8},{8,0},{16,24},{24,16},{32,40},{40,32},{48,56},{56,48},{64,72... | collective-permute-start | bytes 737288 | tf_op jit(solution)/shard_map/ppermute | solution.py:282

commit v4 on v3

--- a/solution.py
+++ b/solution.py
@@ -27,7 +27,11 @@
 ROWS = 2048
 EDGE_AXES = ("x", "z1", "z0", "y")
 NEAR = ("x", "z0", "y", "c")
-DEPTH = ("z1", "zh")
+DEPTH = ("zh", "z1")
+FAR = (((5, 0), (4, 1)), ((4, 0), (5, 1)))
+SIDE = ((7, 6), (3, 2))
+CLOSE = (((6, 1), (2, 0)), ((6, 0), (2, 1)), ((1, 0), (0, 1)))
+SPREAD = (((0, 2), (1, 3)), ((1, 7), (3, 5)), ((2, 4), (7, 6)))
 
 
 def nt(a, b):
@@ -209,14 +213,41 @@
     return jnp.where(is_last, special, out)
 
 
-def sum_kernel(in_ref, out_ref):
+def in_last():
+    return flat_index(NEAR) == math.prod(lax.axis_size(a) for a in NEAR) - 1
+
+
+def pass_on(value, pairs):
+    outer, inner = (lax.axis_size(a) for a in DEPTH)
+    place = [(d % inner) * outer + d // inner for d in range(outer * inner)]
+    return lax.ppermute(value, DEPTH[::-1], [(place[i], place[j]) for i, j in pairs])
+
+
+def plane_sum_kernel(in_ref, out_ref):
     total = in_ref[0].astype(F32)
     for k in range(1, in_ref.shape[0]):
         total = total + in_ref[k].astype(F32)
-    count = math.prod(lax.axis_size(a) for a in NEAR)
-    res = split_sums(total, flat_index(NEAR) == count - 1)
+    out_ref[...] = split_sums(total, in_last())
+
+
+def depth_sum_kernel(*refs):
+    *in_refs, out_ref = refs
+    total = in_refs[0][...].astype(F32)
+    for ref in in_refs[1:]:
+        total = total + ref[...].astype(F32)
+    out_ref[...] = jnp.where(flat_index(DEPTH) < 2, split_sums(total, in_last()), jnp.zeros_like(out_ref))
+
+
+def side_sum_kernel(part_ref, side_ref, out_ref):
+    total = part_ref[...].astype(F32) + side_ref[...].astype(F32)
+    at = flat_index(DEPTH)
+    out_ref[...] = jnp.where((at == 2) | (at == 6), split_sums(total, in_last()), part_ref[...])
+
+
+def copies_kernel(one_ref, two_ref, out_ref):
+    either = one_ref[...] + two_ref[...]
     for k in range(out_ref.shape[0]):
-        out_ref[k] = res
+        out_ref[k] = either
 
 
 def unpack_kernel(in_ref, gw_ref, gb_ref, go_ref, gob_ref):
@@ -289,22 +320,29 @@
     decoded, packed = k1_call(n_rows, scale)(own, pair, wt, conv_bias[:, None], wo, ob, tgt)
 
     near = math.prod(lax.axis_size(a) for a in NEAR)
-    depth = math.prod(lax.axis_size(a) for a in DEPTH)
     chunk = ROWS // near
 
-    def summed(parts, copies):
+    def small(kernel, name, copies, *operands):
         return pl.pallas_call(
-            sum_kernel,
-            out_shape=jax.ShapeDtypeStruct((copies, chunk, W), BF),
-            in_specs=[VM()],
+            kernel,
+            out_shape=jax.ShapeDtypeStruct(copies + (chunk, W), BF),
+            in_specs=[VM()] * len(operands),
             out_specs=VM(),
             compiler_params=pltpu.CompilerParams(vmem_limit_bytes=SMALL),
-            name="sum_parts",
-        )(parts)
+            name=name,
+        )(*operands)
 
     parts = lax.all_to_all(packed.reshape(near, chunk, W), NEAR, 0, 0)
-    parts = lax.all_to_all(summed(parts, depth), DEPTH, 0, 0)
-    parts = lax.all_to_all(summed(parts, near), NEAR, 0, 0)
+    part = small(plane_sum_kernel, "plane_sum", (), parts)
+    side = pass_on(part, SIDE)
+    more = small(side_sum_kernel, "side_sum", (), part, side)
+    close = [pass_on(more, pairs) for pairs in CLOSE[::-1]]
+    far = [pass_on(part, pairs) for pairs in FAR[::-1]]
+    total = small(depth_sum_kernel, "depth_sum", (), part, *close, *far)
+    for pairs in SPREAD[:-1]:
+        total = total + pass_on(total, pairs)
+    outer = pass_on(total, SPREAD[-1])
+    parts = lax.all_to_all(small(copies_kernel, "copies", (near,), total, outer), NEAR, 0, 0)
 
     gw, gb, go, gob = pl.pallas_call(
         unpack_kernel,

time: 88.5 us -> 85.3 us (0.964)
  blocking collectives: 69.1 us -> 45.1 us
  starting transfers between devices: 7.24 us -> 20.5 us
  waiting for transfers between devices: 0.01 us -> 7.14 us
    all_to_all x2 -> x1, blocking collectives: 43.1 us -> 19.2 us  [local(): lax.all_to_all(small(copies_kernel, 'copies', (near,), total, outer), NEA...]
    ppermute x0 -> x9, starting transfers between devices: none -> 13.2 us  [pass_on(): lax.ppermute(value, DEPTH[::-1], [(place[i], place[j]) for i, j in pairs])]
    ppermute x0 -> x9, waiting for transfers between devices: none -> 7.13 us  [pass_on(): lax.ppermute(value, DEPTH[::-1], [(place[i], place[j]) for i, j in pairs])]
  transfers between devices with their start and end apart: 2 -> 11, of which waited for: 0 -> 4; matrix products, arithmetic and copies ran while one was open for 4% -> 4% of each run, Pallas kernels for 0% -> 0%
where the time goes in v4:
time: 85.3 us; the launch traced here: 84.7 us
  blocking collectives  45.1 us (53%)
  starting transfers between devices  20.5 us (24%)
  waiting for transfers between devices  7.14 us (8%)
  Pallas kernels  6.47 us (8%)
  local copies, waits for them, and re-layouts  4.62 us (5%)
    all_to_all x1, blocking collectives, local(): parts = lax.all_to_all(packed.reshape(near, chunk, W), NEAR, 0, 0)  25.9 us
    all_to_all x1, blocking collectives, local(): lax.all_to_all(small(copies_kernel, 'copies', (near,), total, outer), NEA...  19.2 us
    ppermute x9, starting transfers between devices, pass_on(): lax.ppermute(value, DEPTH[::-1], [(place[i], place[j]) for i, j in pairs])  13.2 us
    ppermute x9, waiting for transfers between devices, pass_on(): lax.ppermute(value, DEPTH[::-1], [(place[i], place[j]) for i, j in pairs])  7.13 us
    ppermute x1, starting transfers between devices, local(): lax.ppermute(own, EDGE_AXES, even)  6.56 us
    pallas_call x1, Pallas kernels, local(): k1_call(n_rows, scale)(own, pair, wt, conv_bias[:, None], wo, ob, tgt)  4.96 us
  transfers between devices with their start and end apart: 11, of which 4 were waited for; matrix products, arithmetic and copies ran while one was open for 4% of the time, Pallas kernels for 0%

profile of v4, /device:TPU:1, one launch (start us, length us, event | category | flops | bytes accessed | tf_op | source)
XLA Modules:
  0.0 84.7 jit_solution(8623336323739919509)
XLA Ops:
  0.6 0.0 copy-start
  0.6 1.0 %copy.16 = bf16[1,96,5,2,128]{4,1,3,2,0:T(8,128)(2,1)S(1)} copy(bf16[1,96,5,2,128]{4,3,2,1,0:T(2,128)(2,1)} %param.6) | data formatting | bytes 491520 | tf_op args[0]
  1.6 0.7 collective-permute-start.1
  2.3 6.6 %collective-permute-start = (bf16[5,2,96,128]{3,2,1,0:T(8,128)(2,1)S(1)}, bf16[5,2,96,128]{3,2,1,0:T(8,128)(2,1)S(1)}, u32[]{:S(2)}, u32[]{:S(2)}) collective-permute-start(bf16[5,2,96,128]{3,2,1,0:T(8,128)(2,1)S(1)} %bitcast.22), channel_id=1, source_target_pairs={{0,8},{8,0},{16,24},{24,16},{32,40},{40,32},{48,56},{56,48},{64,72... | collective-permute-start | bytes 737288 | tf_op jit(solution)/shard_map/ppermute | solution.py:313
  8.9 0.7 copy.13
  9.6 0.7 convert_element_type.10
  10.3 0.8 copy.14.cb_ref
  11.1 1.4 %copy.12 = bf16[3,864,96]{1,2,0:T(8,128)(2,1)S(1)} copy(bf16[3,864,96]{2,1,0:T(8,128)(2,1)} %bitcast.26) | data formatting | bytes 995328 | tf_op jit(solution)/shard_map/reshape | solution.py:315
  12.5 0.0 copy-done
  12.6 0.0 collective-permute-done.1
  12.6 0.0 collective-permute-done
  12.6 5.0 %device_part.1 = (bf16[1,3,5,2,128]{4,3,2,1,0:T(2,128)(2,1)}, bf16[2048,128]{1,0:T(8,128)(2,1)S(1)}) custom-call(bf16[5,2,96,128]{3,2,1,0:T(8,128)(2,1)S(1)} %bitcast.23, bf16[2,5,2,96,128]{4,3,2,1,0:T(8,128)(2,1)S(1)} %pad_maximum_fusion.pair_ref, bf16[288,864]{1,0:T(8,128)(2,1)S(1)} %bitcast.20, f32[96,1]{1,0:T(8,128)S(1)} %copy.14.cb_ref, ...), custom_call_target="tpu_custom_call" | custom-call | tf_op jit(solution)/shard_map/device_part/pallas_call | solution.py:320
  17.6 25.9 %all_to_all.10.in_ref = bf16[64,32,128]{2,1,0:T(8,128)(2,1)S(1)} all-to-all(bf16[64,32,128]{2,1,0:T(8,128)(2,1)S(1)} %bitcast.24), channel_id=1, replica_groups=mesh['x'=4,'z1'=2,'z0'=2,'y'=4,'zh'=4,'c'=2] {'x','z0','y','c'}, dimensions={0} | all-to-all | bytes 1048576 | tf_op jit(solution)/shard_map/all_to_all | solution.py:335
  43.5 0.1 plane_sum.1.part_ref.refs_0_
  43.6 0.7 collective-permute-start.2
  44.3 1.3 %collective-permute-start.7 = (bf16[32,128]{1,0:T(8,128)(2,1)S(1)}, bf16[32,128]{1,0:T(8,128)(2,1)S(1)}, u32[]{:S(2)}, u32[]{:S(2)}) collective-permute-start(bf16[32,128]{1,0:T(8,128)(2,1)S(1)} %plane_sum.1.part_ref.refs_0_), channel_id=1, source_target_pairs={{68,0},{4,64},{69,1},{5,65},{76,8},{12,72},{77,9},{13,73},{84,16},... | collective-permute-start | bytes 24584 | tf_op jit(solution)/shard_map/ppermute | solution.py:223
  45.6 1.3 %collective-permute-start.6 = (bf16[32,128]{1,0:T(8,128)(2,1)S(1)}, bf16[32,128]{1,0:T(8,128)(2,1)S(1)}, u32[]{:S(2)}, u32[]{:S(2)}) collective-permute-start(bf16[32,128]{1,0:T(8,128)(2,1)S(1)} %plane_sum.1.part_ref.refs_0_), channel_id=1, source_target_pairs={{4,0},{68,64},{5,1},{69,65},{12,8},{76,72},{13,9},{77,73},{20,16},... | collective-permute-start | bytes 24584 | tf_op jit(solution)/shard_map/ppermute | solution.py:223
  46.9 0.0 collective-permute-done.2.side_ref
  46.9 1.3 %collective-permute-start.5 = (bf16[32,128]{1,0:T(8,128)(2,1)S(1)}, bf16[32,128]{1,0:T(8,128)(2,1)S(1)}, u32[]{:S(2)}, u32[]{:S(2)}) collective-permute-start(bf16[32,128]{1,0:T(8,128)(2,1)S(1)} %side_sum.1), channel_id=1, source_target_pairs={{6,64},{2,0},{7,65},{3,1},{14,72},{10,8},{15,73},{11,9},{22,80},{1... | collective-permute-start | bytes 24584 | tf_op jit(solution)/shard_map/ppermute | solution.py:223
  48.2 1.3 %collective-permute-start.4 = (bf16[32,128]{1,0:T(8,128)(2,1)S(1)}, bf16[32,128]{1,0:T(8,128)(2,1)S(1)}, u32[]{:S(2)}, u32[]{:S(2)}) collective-permute-start(bf16[32,128]{1,0:T(8,128)(2,1)S(1)} %side_sum.1), channel_id=1, source_target_pairs={{6,0},{2,64},{7,1},{3,65},{14,8},{10,72},{15,9},{11,73},{22,16},{1... | collective-permute-start | bytes 24584 | tf_op jit(solution)/shard_map/ppermute | solution.py:223
  49.5 4.8 %collective-permute-start.3 = (bf16[32,128]{1,0:T(8,128)(2,1)S(1)}, bf16[32,128]{1,0:T(8,128)(2,1)S(1)}, u32[]{:S(2)}, u32[]{:S(2)}) collective-permute-start(bf16[32,128]{1,0:T(8,128)(2,1)S(1)} %side_sum.1), channel_id=1, source_target_pairs={{64,0},{0,64},{65,1},{1,65},{72,8},{8,72},{73,9},{9,73},{80,16},{1... | collective-permute-start | bytes 24584 | tf_op jit(solution)/shard_map/ppermute | solution.py:223
  54.4 3.9 %collective-permute-done.7.refs_5_ = bf16[32,128]{1,0:T(8,128)(2,1)S(1)} collective-permute-done((bf16[32,128]{1,0:T(8,128)(2,1)S(1)}, bf16[32,128]{1,0:T(8,128)(2,1)S(1)}, u32[]{:S(2)}, u32[]{:S(2)}) %collective-permute-start.7) | collective-permute-done | bytes 8224 | tf_op jit(solution)/shard_map/ppermute | solution.py:223
  58.3 1.2 %collective-permute-done.6.refs_4_ = bf16[32,128]{1,0:T(8,128)(2,1)S(1)} collective-permute-done((bf16[32,128]{1,0:T(8,128)(2,1)S(1)}, bf16[32,128]{1,0:T(8,128)(2,1)S(1)}, u32[]{:S(2)}, u32[]{:S(2)}) %collective-permute-start.6) | collective-permute-done | bytes 8224 | tf_op jit(solution)/shard_map/ppermute | solution.py:223
  59.5 0.0 collective-permute-done.5.refs_3_
  59.5 1.2 %collective-permute-done.4.refs_2_ = bf16[32,128]{1,0:T(8,128)(2,1)S(1)} collective-permute-done((bf16[32,128]{1,0:T(8,128)(2,1)S(1)}, bf16[32,128]{1,0:T(8,128)(2,1)S(1)}, u32[]{:S(2)}, u32[]{:S(2)}) %collective-permute-start.4) | collective-permute-done | bytes 8224 | tf_op jit(solution)/shard_map/ppermute | solution.py:223
  60.7 0.0 collective-permute-done.3.refs_1_
  60.7 1.3 %collective-permute-start.8 = (bf16[32,128]{1,0:T(8,128)(2,1)S(1)}, bf16[32,128]{1,0:T(8,128)(2,1)S(1)}, u32[]{:S(2)}, u32[]{:S(2)}) collective-permute-start(bf16[32,128]{1,0:T(8,128)(2,1)S(1)} %depth_sum.1), channel_id=1, source_target_pairs={{0,2},{64,66},{1,3},{65,67},{8,10},{72,74},{9,11},{73,75},{16,18},... | collective-permute-start | bytes 24584 | tf_op jit(solution)/shard_map/ppermute | solution.py:223
  62.0 0.8 collective-permute-done.8
  62.8 0.6 collective-permute-start.9
  63.5 0.0 collective-permute-done.9
  63.5 0.7 collective-permute-start.10
  64.2 0.0 collective-permute-done.10.two_ref
  64.2 19.2 %all_to_all.11 = bf16[64,32,128]{2,1,0:T(8,128)(2,1)S(1)} all-to-all(bf16[64,32,128]{2,1,0:T(8,128)(2,1)S(1)} %copies.1), channel_id=1, replica_groups=mesh['x'=4,'z1'=2,'z0'=2,'y'=4,'zh'=4,'c'=2] {'x','z0','y','c'}, dimensions={0} | all-to-all | bytes 1048576 | tf_op jit(solution)/shard_map/all_to_all | solution.py:345
  83.4 1.3 %unpack.1 = (f32[2592,96]{1,0:T(8,128)}, f32[96]{0:T(128)}, f32[3,27,96]{2,1,0:T(8,128)}, f32[3]{0:T(128)}) custom-call(bf16[2048,128]{1,0:T(8,128)(2,1)S(1)} %bitcast.19), custom_call_target="tpu_custom_call" | custom-call | tf_op jit(solution)/shard_map/unpack/pallas_call | solution.py:347
  (9 shorter events, 0.2 us)
Async XLA Ops:
  0.6 11.9 %copy-start = (bf16[27,96,3]{1,0,2:T(8,128)(2,1)S(1)}, bf16[27,96,3]{1,0,2:T(8,128)(2,1)}, u32[]{:S(2)}) copy-start(bf16[27,96,3]{1,0,2:T(8,128)(2,1)} %param.9) | copy-start | bytes 46660
  1.6 10.9 %collective-permute-start.1 = (bf16[5,2,96,128]{3,2,1,0:T(8,128)(2,1)S(1)}, bf16[5,2,96,128]{3,2,1,0:T(8,128)(2,1)S(1)}, u32[]{:S(2)}, u32[]{:S(2)}) collective-permute-start(bf16[5,2,96,128]{3,2,1,0:T(8,128)(2,1)S(1)} %bitcast.21), channel_id=1, source_target_pairs={{8,16},{16,8},{24,32},{32,24},{40,48},{48,40},{56,64},{64,56},{72,... | collective-permute-start | bytes 737288 | tf_op jit(solution)/shard_map/ppermute | solution.py:313
  2.3 10.3 %collective-permute-start = (bf16[5,2,96,128]{3,2,1,0:T(8,128)(2,1)S(1)}, bf16[5,2,96,128]{3,2,1,0:T(8,128)(2,1)S(1)}, u32[]{:S(2)}, u32[]{:S(2)}) collective-permute-start(bf16[5,2,96,128]{3,2,1,0:T(8,128)(2,1)S(1)} %bitcast.22), channel_id=1, source_target_pairs={{0,8},{8,0},{16,24},{24,16},{32,40},{40,32},{48,56},{56,48},{64,72... | collective-permute-start | bytes 737288 | tf_op jit(solution)/shard_map/ppermute | solution.py:313
  43.6 3.3 %collective-permute-start.2 = (bf16[32,128]{1,0:T(8,128)(2,1)S(1)}, bf16[32,128]{1,0:T(8,128)(2,1)S(1)}, u32[]{:S(2)}, u32[]{:S(2)}) collective-permute-start(bf16[32,128]{1,0:T(8,128)(2,1)S(1)} %plane_sum.1.part_ref.refs_0_), channel_id=1, source_target_pairs={{70,6},{66,2},{71,7},{67,3},{78,14},{74,10},{79,15},{75,11},{86,22... | collective-permute-start | bytes 24584 | tf_op jit(solution)/shard_map/ppermute | solution.py:223
  44.3 14.0 %collective-permute-start.7 = (bf16[32,128]{1,0:T(8,128)(2,1)S(1)}, bf16[32,128]{1,0:T(8,128)(2,1)S(1)}, u32[]{:S(2)}, u32[]{:S(2)}) collective-permute-start(bf16[32,128]{1,0:T(8,128)(2,1)S(1)} %plane_sum.1.part_ref.refs_0_), channel_id=1, source_target_pairs={{68,0},{4,64},{69,1},{5,65},{76,8},{12,72},{77,9},{13,73},{84,16},... | collective-permute-start | bytes 24584 | tf_op jit(solution)/shard_map/ppermute | solution.py:223
  45.6 13.9 %collective-permute-start.6 = (bf16[32,128]{1,0:T(8,128)(2,1)S(1)}, bf16[32,128]{1,0:T(8,128)(2,1)S(1)}, u32[]{:S(2)}, u32[]{:S(2)}) collective-permute-start(bf16[32,128]{1,0:T(8,128)(2,1)S(1)} %plane_sum.1.part_ref.refs_0_), channel_id=1, source_target_pairs={{4,0},{68,64},{5,1},{69,65},{12,8},{76,72},{13,9},{77,73},{20,16},... | collective-permute-start | bytes 24584 | tf_op jit(solution)/shard_map/ppermute | solution.py:223
  46.9 12.6 %collective-permute-start.5 = (bf16[32,128]{1,0:T(8,128)(2,1)S(1)}, bf16[32,128]{1,0:T(8,128)(2,1)S(1)}, u32[]{:S(2)}, u32[]{:S(2)}) collective-permute-start(bf16[32,128]{1,0:T(8,128)(2,1)S(1)} %side_sum.1), channel_id=1, source_target_pairs={{6,64},{2,0},{7,65},{3,1},{14,72},{10,8},{15,73},{11,9},{22,80},{1... | collective-permute-start | bytes 24584 | tf_op jit(solution)/shard_map/ppermute | solution.py:223
  48.2 12.5 %collective-permute-start.4 = (bf16[32,128]{1,0:T(8,128)(2,1)S(1)}, bf16[32,128]{1,0:T(8,128)(2,1)S(1)}, u32[]{:S(2)}, u32[]{:S(2)}) collective-permute-start(bf16[32,128]{1,0:T(8,128)(2,1)S(1)} %side_sum.1), channel_id=1, source_target_pairs={{6,0},{2,64},{7,1},{3,65},{14,8},{10,72},{15,9},{11,73},{22,16},{1... | collective-permute-start | bytes 24584 | tf_op jit(solution)/shard_map/ppermute | solution.py:223
  49.5 11.2 %collective-permute-start.3 = (bf16[32,128]{1,0:T(8,128)(2,1)S(1)}, bf16[32,128]{1,0:T(8,128)(2,1)S(1)}, u32[]{:S(2)}, u32[]{:S(2)}) collective-permute-start(bf16[32,128]{1,0:T(8,128)(2,1)S(1)} %side_sum.1), channel_id=1, source_target_pairs={{64,0},{0,64},{65,1},{1,65},{72,8},{8,72},{73,9},{9,73},{80,16},{1... | collective-permute-start | bytes 24584 | tf_op jit(solution)/shard_map/ppermute | solution.py:223
  60.7 2.1 %collective-permute-start.8 = (bf16[32,128]{1,0:T(8,128)(2,1)S(1)}, bf16[32,128]{1,0:T(8,128)(2,1)S(1)}, u32[]{:S(2)}, u32[]{:S(2)}) collective-permute-start(bf16[32,128]{1,0:T(8,128)(2,1)S(1)} %depth_sum.1), channel_id=1, source_target_pairs={{0,2},{64,66},{1,3},{65,67},{8,10},{72,74},{9,11},{73,75},{16,18},... | collective-permute-start | bytes 24584 | tf_op jit(solution)/shard_map/ppermute | solution.py:223
  62.8 0.7 collective-permute-start.9
  63.5 0.7 collective-permute-start.10

commit v5 on v4

--- a/solution.py
+++ b/solution.py
@@ -25,6 +25,7 @@
 MAIN = 1920
 TAIL = NW - MAIN
 ROWS = 2048
+AXES = ("x", "z1", "z0", "y", "zh", "c")
 EDGE_AXES = ("x", "z1", "z0", "y")
 NEAR = ("x", "z0", "y", "c")
 DEPTH = ("zh", "z1")
@@ -54,6 +55,24 @@
     return jnp.where(lane > 0, pltpu.roll(v, 1, 1), 0.0)
 
 
+FIRST = 33
+
+
+def scatter_groups():
+    nx, nz1, nz0, ny, nzh, nc = (lax.axis_size(a) for a in AXES)
+    groups = []
+    for z1 in range(nz1):
+        for zh in range(nzh):
+            members = []
+            for place in range(nx * nz0 * ny * nc):
+                rest, c = divmod(place ^ FIRST, nc)
+                rest, y = divmod(rest, ny)
+                x, z0 = divmod(rest, nz0)
+                members.append(((((x * nz1 + z1) * nz0 + z0) * ny + y) * nzh + zh) * nc + c)
+            groups.append(members)
+    return groups
+
+
 def flat_index(axes):
     index = 0
     for axis in axes:
@@ -64,7 +83,7 @@
 def device_kernel(
     n_rows, scale,
     own_ref, pair_ref, wt_ref, cb_ref, wo_ref, ob_ref, tgt_ref,
-    dec_ref, pay_ref,
+    dec_ref, out_ref,
     q_ref, r_ref, hid_ref, fac_ref, y_ref, g_ref, gh_ref, main_ref,
 ):
     row_id = flat_index(EDGE_AXES)
@@ -74,6 +93,7 @@
     lane96 = lax.broadcasted_iota(jnp.int32, (C, W), 1)
     lane8 = lax.broadcasted_iota(jnp.int32, (OPAD, W), 1)
 
+    q_ref[KT:, :] = jnp.ones((16, POS), BF)
     for g in range(F):
         for r in range(6):
             if r < 2:
@@ -103,7 +123,7 @@
     keep = jnp.where(outside, 0.0, 1.0)
     def conv(f):
         low = max(0, f - 2) * C
-        r_ref[f, low:, :] = nn(wt_ref[low:, :], q_ref[:, f * FW : (f + 1) * FW])
+        r_ref[f, low:, :] = nn(wt_ref[low:, :], q_ref[:KT, f * FW : (f + 1) * FW])
 
     def activate(f):
         pre = cb_ref[...]
@@ -177,28 +197,31 @@
             gh_ref[W : W + C, (f - 1) * FW : f * FW] = gh
 
     both = nt(q_ref[...], gh_ref[...])
-    main_ref[2 * KT :, :] = both[:, :W]
-    main_ref[KT : 2 * KT, :] = both[:, W:]
-    main_ref[:KT, :] = nt(q_ref[:, : 3 * FW], gh_ref[:W, 2 * FW :])
+    main_ref[2 * KT : NW, :] = both[:KT, :W]
+    main_ref[NW:, :] = both[KT:, :W]
+    main_ref[KT : 2 * KT, :] = both[:KT, W:]
+    main_ref[:KT, :] = nt(q_ref[:KT, : 3 * FW], gh_ref[:W, 2 * FW :])
     gow = nt(g_ref[...], hid_ref[...]).astype(BF)
     gow = nn(pick, gow)
-    bias = nt(jnp.ones((OPAD, POS), BF), gh_ref[:W, :])
+    bias = main_ref[NW : NW + OPAD, :]
     obias = jnp.broadcast_to(jnp.sum(obsum, axis=1, keepdims=True), (OPAD, W))
 
     lane = lax.broadcasted_iota(jnp.int32, (TAIL, W), 1)
     for k in range(3):
         lo, hi = k * TAIL, (k + 1) * TAIL
-        tail = pltpu.roll(main_ref[MAIN:, :], 96 - 32 * k, 1)
+        tail = pltpu.roll(main_ref[MAIN:NW, :], 96 - 32 * k, 1)
         if hi <= MAIN:
             head = main_ref[lo:hi, :]
         else:
             head = jnp.concatenate(
                 [main_ref[lo:MAIN, :], jnp.pad(gow, ((0, 0), (0, W - C)))], axis=0
             )
-        pay_ref[lo:hi, :] = jnp.where(lane < C, head, tail).astype(BF)
-    for at, v in ((2016, bias), (2032, obias)):
+        out_ref[lo:hi, :] = jnp.where(lane < C, head, tail).astype(BF)
+    ends = []
+    for v in (bias, obias):
         top = v.astype(BF).astype(F32)
-        pay_ref[at : at + 16, :] = jnp.concatenate([top, v - top], axis=0).astype(BF)
+        ends += [top, v - top]
+    out_ref[ROWS - 32 :, :] = jnp.concatenate(ends, axis=0).astype(BF)
 
 
 def split_sums(total, is_last):
@@ -214,7 +237,8 @@
 
 
 def in_last():
-    return flat_index(NEAR) == math.prod(lax.axis_size(a) for a in NEAR) - 1
+    last = math.prod(lax.axis_size(a) for a in NEAR) - 1
+    return flat_index(NEAR) == last ^ FIRST
 
 
 def pass_on(value, pairs):
@@ -287,14 +311,14 @@
         in_specs=[VM()] * 7,
         out_specs=(VM(), VM()),
         scratch_shapes=[
-            pltpu.VMEM((KT, POS), BF),
+            pltpu.VMEM((KT + 16, POS), BF),
             pltpu.VMEM((F, 3 * C, FW), F32),
             pltpu.VMEM((C, POS), BF),
             pltpu.VMEM((C, POS), F32),
             pltpu.VMEM((GROWS, POS), F32),
             pltpu.VMEM((GROWS, POS), BF),
             pltpu.VMEM((2 * W, POS), BF),
-            pltpu.VMEM((NW, W), F32),
+            pltpu.VMEM((NW + 16, W), F32),
         ],
         compiler_params=pltpu.CompilerParams(vmem_limit_bytes=LIMIT),
         name="device_part",
@@ -304,6 +328,7 @@
 def local(latent_features, conv_weight, conv_bias, out_weight, out_bias, target_frames):
     sizes = [lax.axis_size(a) for a in EDGE_AXES]
     n_rows = math.prod(sizes)
+    near = math.prod(lax.axis_size(a) for a in NEAR)
     clips = lax.axis_size("zh") * lax.axis_size("c")
     scale = 1.0 / math.sqrt(3 * clips * F * 2 * n_rows * W)
 
@@ -319,7 +344,6 @@
 
     decoded, packed = k1_call(n_rows, scale)(own, pair, wt, conv_bias[:, None], wo, ob, tgt)
 
-    near = math.prod(lax.axis_size(a) for a in NEAR)
     chunk = ROWS // near
 
     def small(kernel, name, copies, *operands):
@@ -332,7 +356,7 @@
             name=name,
         )(*operands)
 
-    parts = lax.all_to_all(packed.reshape(near, chunk, W), NEAR, 0, 0)
+    parts = lax.all_to_all(packed.reshape(near, chunk, W), AXES, 0, 0, axis_index_groups=scatter_groups())
     part = small(plane_sum_kernel, "plane_sum", (), parts)
     side = pass_on(part, SIDE)
     more = small(side_sum_kernel, "side_sum", (), part, side)
@@ -342,7 +366,8 @@
     for pairs in SPREAD[:-1]:
         total = total + pass_on(total, pairs)
     outer = pass_on(total, SPREAD[-1])
-    parts = lax.all_to_all(small(copies_kernel, "copies", (near,), total, outer), NEAR, 0, 0)
+    parts = small(copies_kernel, "copies", (near,), total, outer)
+    parts = lax.all_to_all(parts, AXES, 0, 0, axis_index_groups=scatter_groups())
 
     gw, gb, go, gob = pl.pallas_call(
         unpack_kernel,
@@ -367,7 +392,7 @@
 
 
 def solution(mesh):
-    split = Mesh(mesh.devices.reshape(4, 2, 2, 4, 4, 2), ("x", "z1", "z0", "y", "zh", "c"))
+    split = Mesh(mesh.devices.reshape(4, 2, 2, 4, 4, 2), AXES)
     frames = P(("zh", "c"), None, None, EDGE_AXES, None)
     return jax.shard_map(
         local,

time: 85.3 us -> 83.3 us (0.977)
  blocking collectives: 45.1 us -> 43.3 us
  starting transfers between devices: 20.5 us -> 19.6 us
    all_to_all x2, blocking collectives: 45.1 us -> 43.3 us  [the longest x1 24.3 us: local(): lax.all_to_all(packed.reshape(near, chunk, W), AXES, 0, 0, axis_index_gro...]
    ppermute x9, starting transfers between devices: 13.2 us -> 12.3 us  [pass_on(): lax.ppermute(value, DEPTH[::-1], [(place[i], place[j]) for i, j in pairs])]
where the time goes in v5:
time: 83.3 us; the launch traced here: 82.6 us
  blocking collectives  43.3 us (52%)
  starting transfers between devices  19.6 us (24%)
  waiting for transfers between devices  7.78 us (9%)
  Pallas kernels  6.44 us (8%)
  local copies, waits for them, and re-layouts  4.62 us (6%)
  between operations  0.85 us (1%)
    all_to_all x1, blocking collectives, local(): lax.all_to_all(packed.reshape(near, chunk, W), AXES, 0, 0, axis_index_gro...  24.3 us
    all_to_all x1, blocking collectives, local(): lax.all_to_all(parts, AXES, 0, 0, axis_index_groups=scatter_groups())  19 us
    ppermute x9, starting transfers between devices, pass_on(): lax.ppermute(value, DEPTH[::-1], [(place[i], place[j]) for i, j in pairs])  12.3 us
    ppermute x9, waiting for transfers between devices, pass_on(): lax.ppermute(value, DEPTH[::-1], [(place[i], place[j]) for i, j in pairs])  7.78 us
    ppermute x1, starting transfers between devices, local(): lax.ppermute(own, EDGE_AXES, even)  6.56 us
    pallas_call x1, Pallas kernels, local(): k1_call(n_rows, scale)(own, pair, wt, conv_bias[:, None], wo, ob, tgt)  4.93 us
  transfers between devices with their start and end apart: 11, of which 4 were waited for; matrix products, arithmetic and copies ran while one was open for 4% of the time, Pallas kernels for 0%

profile of v5, /device:TPU:1, one launch (start us, length us, event | category | flops | bytes accessed | tf_op | source)
XLA Modules:
  0.0 82.6 jit_solution(13532596221416609604)
XLA Ops:
  0.6 0.0 copy-start
  0.6 1.0 %copy.16 = bf16[1,96,5,2,128]{4,1,3,2,0:T(8,128)(2,1)S(1)} copy(bf16[1,96,5,2,128]{4,3,2,1,0:T(2,128)(2,1)} %param.6) | data formatting | bytes 491520 | tf_op args[0]
  1.6 0.7 collective-permute-start.1
  2.3 6.6 %collective-permute-start = (bf16[5,2,96,128]{3,2,1,0:T(8,128)(2,1)S(1)}, bf16[5,2,96,128]{3,2,1,0:T(8,128)(2,1)S(1)}, u32[]{:S(2)}, u32[]{:S(2)}) collective-permute-start(bf16[5,2,96,128]{3,2,1,0:T(8,128)(2,1)S(1)} %bitcast.22), channel_id=1, source_target_pairs={{0,8},{8,0},{16,24},{24,16},{32,40},{40,32},{48,56},{56,48},{64,72... | collective-permute-start | bytes 737288 | tf_op jit(solution)/shard_map/ppermute | solution.py:338
  8.9 0.7 copy.13
  9.6 0.7 convert_element_type.10
  10.3 0.8 copy.14.cb_ref
  11.1 1.4 %copy.12 = bf16[3,864,96]{1,2,0:T(8,128)(2,1)S(1)} copy(bf16[3,864,96]{2,1,0:T(8,128)(2,1)} %bitcast.26) | data formatting | bytes 995328 | tf_op jit(solution)/shard_map/reshape | solution.py:340
  12.5 0.0 copy-done
  12.6 0.0 collective-permute-done.1
  12.6 0.0 collective-permute-done
  12.6 4.9 %device_part.1 = (bf16[1,3,5,2,128]{4,3,2,1,0:T(2,128)(2,1)}, bf16[2048,128]{1,0:T(8,128)(2,1)S(1)}) custom-call(bf16[5,2,96,128]{3,2,1,0:T(8,128)(2,1)S(1)} %bitcast.23, bf16[2,5,2,96,128]{4,3,2,1,0:T(8,128)(2,1)S(1)} %pad_maximum_fusion.pair_ref, bf16[288,864]{1,0:T(8,128)(2,1)S(1)} %bitcast.20, f32[96,1]{1,0:T(8,128)S(1)} %copy.14.cb_ref, ...), custom_call_target="tpu_custom_call" | custom-call | tf_op jit(solution)/shard_map/device_part/pallas_call | solution.py:345
  17.6 24.3 %all_to_all.10.in_ref = bf16[64,32,128]{2,1,0:T(8,128)(2,1)S(1)} all-to-all(bf16[64,32,128]{2,1,0:T(8,128)(2,1)S(1)} %bitcast.24), channel_id=1, replica_groups={{257,256,265,264,273,272,281,280,289,288,297,296,305,304,313,312,385,38..., dimensions={0} | all-to-all | bytes 1048576 | tf_op jit(solution)/shard_map/all_to_all | solution.py:359
  41.8 0.1 plane_sum.1.part_ref.refs_0_
  41.9 0.7 collective-permute-start.2
  42.6 1.3 %collective-permute-start.7 = (bf16[32,128]{1,0:T(8,128)(2,1)S(1)}, bf16[32,128]{1,0:T(8,128)(2,1)S(1)}, u32[]{:S(2)}, u32[]{:S(2)}) collective-permute-start(bf16[32,128]{1,0:T(8,128)(2,1)S(1)} %plane_sum.1.part_ref.refs_0_), channel_id=1, source_target_pairs={{68,0},{4,64},{69,1},{5,65},{76,8},{12,72},{77,9},{13,73},{84,16},... | collective-permute-start | bytes 24584 | tf_op jit(solution)/shard_map/ppermute | solution.py:247
  43.9 1.3 %collective-permute-start.6 = (bf16[32,128]{1,0:T(8,128)(2,1)S(1)}, bf16[32,128]{1,0:T(8,128)(2,1)S(1)}, u32[]{:S(2)}, u32[]{:S(2)}) collective-permute-start(bf16[32,128]{1,0:T(8,128)(2,1)S(1)} %plane_sum.1.part_ref.refs_0_), channel_id=1, source_target_pairs={{4,0},{68,64},{5,1},{69,65},{12,8},{76,72},{13,9},{77,73},{20,16},... | collective-permute-start | bytes 24584 | tf_op jit(solution)/shard_map/ppermute | solution.py:247
  45.2 0.0 collective-permute-done.2.side_ref
  45.2 1.3 %collective-permute-start.5 = (bf16[32,128]{1,0:T(8,128)(2,1)S(1)}, bf16[32,128]{1,0:T(8,128)(2,1)S(1)}, u32[]{:S(2)}, u32[]{:S(2)}) collective-permute-start(bf16[32,128]{1,0:T(8,128)(2,1)S(1)} %side_sum.1), channel_id=1, source_target_pairs={{6,64},{2,0},{7,65},{3,1},{14,72},{10,8},{15,73},{11,9},{22,80},{1... | collective-permute-start | bytes 24584 | tf_op jit(solution)/shard_map/ppermute | solution.py:247
  46.5 1.3 %collective-permute-start.4 = (bf16[32,128]{1,0:T(8,128)(2,1)S(1)}, bf16[32,128]{1,0:T(8,128)(2,1)S(1)}, u32[]{:S(2)}, u32[]{:S(2)}) collective-permute-start(bf16[32,128]{1,0:T(8,128)(2,1)S(1)} %side_sum.1), channel_id=1, source_target_pairs={{6,0},{2,64},{7,1},{3,65},{14,8},{10,72},{15,9},{11,73},{22,16},{1... | collective-permute-start | bytes 24584 | tf_op jit(solution)/shard_map/ppermute | solution.py:247
  47.8 3.9 %collective-permute-start.3 = (bf16[32,128]{1,0:T(8,128)(2,1)S(1)}, bf16[32,128]{1,0:T(8,128)(2,1)S(1)}, u32[]{:S(2)}, u32[]{:S(2)}) collective-permute-start(bf16[32,128]{1,0:T(8,128)(2,1)S(1)} %side_sum.1), channel_id=1, source_target_pairs={{64,0},{0,64},{65,1},{1,65},{72,8},{8,72},{73,9},{9,73},{80,16},{1... | collective-permute-start | bytes 24584 | tf_op jit(solution)/shard_map/ppermute | solution.py:247
  51.8 3.9 %collective-permute-done.7.refs_5_ = bf16[32,128]{1,0:T(8,128)(2,1)S(1)} collective-permute-done((bf16[32,128]{1,0:T(8,128)(2,1)S(1)}, bf16[32,128]{1,0:T(8,128)(2,1)S(1)}, u32[]{:S(2)}, u32[]{:S(2)}) %collective-permute-start.7) | collective-permute-done | bytes 8224 | tf_op jit(solution)/shard_map/ppermute | solution.py:247
  55.7 1.4 %collective-permute-done.6.refs_4_ = bf16[32,128]{1,0:T(8,128)(2,1)S(1)} collective-permute-done((bf16[32,128]{1,0:T(8,128)(2,1)S(1)}, bf16[32,128]{1,0:T(8,128)(2,1)S(1)}, u32[]{:S(2)}, u32[]{:S(2)}) %collective-permute-start.6) | collective-permute-done | bytes 8224 | tf_op jit(solution)/shard_map/ppermute | solution.py:247
  57.1 0.0 collective-permute-done.5.refs_3_
  57.1 1.7 %collective-permute-done.4.refs_2_ = bf16[32,128]{1,0:T(8,128)(2,1)S(1)} collective-permute-done((bf16[32,128]{1,0:T(8,128)(2,1)S(1)}, bf16[32,128]{1,0:T(8,128)(2,1)S(1)}, u32[]{:S(2)}, u32[]{:S(2)}) %collective-permute-start.4) | collective-permute-done | bytes 8224 | tf_op jit(solution)/shard_map/ppermute | solution.py:247
  58.7 0.0 collective-permute-done.3.refs_1_
  58.8 1.3 %collective-permute-start.8 = (bf16[32,128]{1,0:T(8,128)(2,1)S(1)}, bf16[32,128]{1,0:T(8,128)(2,1)S(1)}, u32[]{:S(2)}, u32[]{:S(2)}) collective-permute-start(bf16[32,128]{1,0:T(8,128)(2,1)S(1)} %depth_sum.1), channel_id=1, source_target_pairs={{0,2},{64,66},{1,3},{65,67},{8,10},{72,74},{9,11},{73,75},{16,18},... | collective-permute-start | bytes 24584 | tf_op jit(solution)/shard_map/ppermute | solution.py:247
  60.1 0.8 collective-permute-done.8
  60.9 0.6 collective-permute-start.9
  61.5 0.0 collective-permute-done.9
  61.5 0.7 collective-permute-start.10
  62.2 0.0 collective-permute-done.10.two_ref
  62.3 19.0 %all_to_all.11 = bf16[64,32,128]{2,1,0:T(8,128)(2,1)S(1)} all-to-all(bf16[64,32,128]{2,1,0:T(8,128)(2,1)S(1)} %copies.1), channel_id=1, replica_groups={{257,256,265,264,273,272,281,280,289,288,297,296,305,304,313,312,385,38..., dimensions={0} | all-to-all | bytes 1048576 | tf_op jit(solution)/shard_map/all_to_all | solution.py:370
  81.3 1.3 %unpack.1 = (f32[2592,96]{1,0:T(8,128)}, f32[96]{0:T(128)}, f32[3,27,96]{2,1,0:T(8,128)}, f32[3]{0:T(128)}) custom-call(bf16[2048,128]{1,0:T(8,128)(2,1)S(1)} %bitcast.19), custom_call_target="tpu_custom_call" | custom-call | tf_op jit(solution)/shard_map/unpack/pallas_call | solution.py:372
  (9 shorter events, 0.2 us)
Async XLA Ops:
  0.6 11.9 %copy-start = (bf16[27,96,3]{1,0,2:T(8,128)(2,1)S(1)}, bf16[27,96,3]{1,0,2:T(8,128)(2,1)}, u32[]{:S(2)}) copy-start(bf16[27,96,3]{1,0,2:T(8,128)(2,1)} %param.9) | copy-start | bytes 46660
  1.6 10.9 %collective-permute-start.1 = (bf16[5,2,96,128]{3,2,1,0:T(8,128)(2,1)S(1)}, bf16[5,2,96,128]{3,2,1,0:T(8,128)(2,1)S(1)}, u32[]{:S(2)}, u32[]{:S(2)}) collective-permute-start(bf16[5,2,96,128]{3,2,1,0:T(8,128)(2,1)S(1)} %bitcast.21), channel_id=1, source_target_pairs={{8,16},{16,8},{24,32},{32,24},{40,48},{48,40},{56,64},{64,56},{72,... | collective-permute-start | bytes 737288 | tf_op jit(solution)/shard_map/ppermute | solution.py:338
  2.3 10.3 %collective-permute-start = (bf16[5,2,96,128]{3,2,1,0:T(8,128)(2,1)S(1)}, bf16[5,2,96,128]{3,2,1,0:T(8,128)(2,1)S(1)}, u32[]{:S(2)}, u32[]{:S(2)}) collective-permute-start(bf16[5,2,96,128]{3,2,1,0:T(8,128)(2,1)S(1)} %bitcast.22), channel_id=1, source_target_pairs={{0,8},{8,0},{16,24},{24,16},{32,40},{40,32},{48,56},{56,48},{64,72... | collective-permute-start | bytes 737288 | tf_op jit(solution)/shard_map/ppermute | solution.py:338
  41.9 3.3 %collective-permute-start.2 = (bf16[32,128]{1,0:T(8,128)(2,1)S(1)}, bf16[32,128]{1,0:T(8,128)(2,1)S(1)}, u32[]{:S(2)}, u32[]{:S(2)}) collective-permute-start(bf16[32,128]{1,0:T(8,128)(2,1)S(1)} %plane_sum.1.part_ref.refs_0_), channel_id=1, source_target_pairs={{70,6},{66,2},{71,7},{67,3},{78,14},{74,10},{79,15},{75,11},{86,22... | collective-permute-start | bytes 24584 | tf_op jit(solution)/shard_map/ppermute | solution.py:247
  42.6 13.1 %collective-permute-start.7 = (bf16[32,128]{1,0:T(8,128)(2,1)S(1)}, bf16[32,128]{1,0:T(8,128)(2,1)S(1)}, u32[]{:S(2)}, u32[]{:S(2)}) collective-permute-start(bf16[32,128]{1,0:T(8,128)(2,1)S(1)} %plane_sum.1.part_ref.refs_0_), channel_id=1, source_target_pairs={{68,0},{4,64},{69,1},{5,65},{76,8},{12,72},{77,9},{13,73},{84,16},... | collective-permute-start | bytes 24584 | tf_op jit(solution)/shard_map/ppermute | solution.py:247
  43.9 13.2 %collective-permute-start.6 = (bf16[32,128]{1,0:T(8,128)(2,1)S(1)}, bf16[32,128]{1,0:T(8,128)(2,1)S(1)}, u32[]{:S(2)}, u32[]{:S(2)}) collective-permute-start(bf16[32,128]{1,0:T(8,128)(2,1)S(1)} %plane_sum.1.part_ref.refs_0_), channel_id=1, source_target_pairs={{4,0},{68,64},{5,1},{69,65},{12,8},{76,72},{13,9},{77,73},{20,16},... | collective-permute-start | bytes 24584 | tf_op jit(solution)/shard_map/ppermute | solution.py:247
  45.2 11.8 %collective-permute-start.5 = (bf16[32,128]{1,0:T(8,128)(2,1)S(1)}, bf16[32,128]{1,0:T(8,128)(2,1)S(1)}, u32[]{:S(2)}, u32[]{:S(2)}) collective-permute-start(bf16[32,128]{1,0:T(8,128)(2,1)S(1)} %side_sum.1), channel_id=1, source_target_pairs={{6,64},{2,0},{7,65},{3,1},{14,72},{10,8},{15,73},{11,9},{22,80},{1... | collective-permute-start | bytes 24584 | tf_op jit(solution)/shard_map/ppermute | solution.py:247
  46.5 12.2 %collective-permute-start.4 = (bf16[32,128]{1,0:T(8,128)(2,1)S(1)}, bf16[32,128]{1,0:T(8,128)(2,1)S(1)}, u32[]{:S(2)}, u32[]{:S(2)}) collective-permute-start(bf16[32,128]{1,0:T(8,128)(2,1)S(1)} %side_sum.1), channel_id=1, source_target_pairs={{6,0},{2,64},{7,1},{3,65},{14,8},{10,72},{15,9},{11,73},{22,16},{1... | collective-permute-start | bytes 24584 | tf_op jit(solution)/shard_map/ppermute | solution.py:247
  47.8 10.9 %collective-permute-start.3 = (bf16[32,128]{1,0:T(8,128)(2,1)S(1)}, bf16[32,128]{1,0:T(8,128)(2,1)S(1)}, u32[]{:S(2)}, u32[]{:S(2)}) collective-permute-start(bf16[32,128]{1,0:T(8,128)(2,1)S(1)} %side_sum.1), channel_id=1, source_target_pairs={{64,0},{0,64},{65,1},{1,65},{72,8},{8,72},{73,9},{9,73},{80,16},{1... | collective-permute-start | bytes 24584 | tf_op jit(solution)/shard_map/ppermute | solution.py:247
  58.8 2.1 %collective-permute-start.8 = (bf16[32,128]{1,0:T(8,128)(2,1)S(1)}, bf16[32,128]{1,0:T(8,128)(2,1)S(1)}, u32[]{:S(2)}, u32[]{:S(2)}) collective-permute-start(bf16[32,128]{1,0:T(8,128)(2,1)S(1)} %depth_sum.1), channel_id=1, source_target_pairs={{0,2},{64,66},{1,3},{65,67},{8,10},{72,74},{9,11},{73,75},{16,18},... | collective-permute-start | bytes 24584 | tf_op jit(solution)/shard_map/ppermute | solution.py:247
  60.9 0.7 collective-permute-start.9
  61.5 0.7 collective-permute-start.10

commit v6 on v5

--- a/solution.py
+++ b/solution.py
@@ -55,7 +55,7 @@
     return jnp.where(lane > 0, pltpu.roll(v, 1, 1), 0.0)
 
 
-FIRST = 33
+FIRST = 41
 
 
 def scatter_groups():
@@ -82,12 +82,12 @@
 
 def device_kernel(
     n_rows, scale,
-    own_ref, pair_ref, wt_ref, cb_ref, wo_ref, ob_ref, tgt_ref,
+    own_ref, one_ref, two_ref, wt_ref, cb_ref, wo_ref, ob_ref, tgt_ref,
     dec_ref, out_ref,
     q_ref, r_ref, hid_ref, fac_ref, y_ref, g_ref, gh_ref, main_ref,
 ):
     row_id = flat_index(EDGE_AXES)
-    odd = lax.rem(row_id, 2)
+    prev_first = lax.rem(row_id + lax.axis_index("c"), 2) == 1
     first = row_id == 0
     last = row_id == n_rows - 1
     lane96 = lax.broadcasted_iota(jnp.int32, (C, W), 1)
@@ -97,11 +97,11 @@
     for g in range(F):
         for r in range(6):
             if r < 2:
-                tile = pair_ref[1 - odd, g, r]
+                tile = jnp.where(prev_first, one_ref[g, r], two_ref[g, r])
             elif r < 4:
                 tile = own_ref[g, r - 2]
             else:
-                tile = pair_ref[odd, g, r - 4]
+                tile = jnp.where(prev_first, two_ref[g, r - 4], one_ref[g, r - 4])
             wide = tile.astype(F32)
             for kj in range(3):
                 piece = tile if kj == 1 else shifted(wide, lane96, kj - 1).astype(BF)
@@ -308,7 +308,7 @@
             jax.ShapeDtypeStruct((1, 3, F, 2, W), BF),
             jax.ShapeDtypeStruct((ROWS, W), BF),
         ),
-        in_specs=[VM()] * 7,
+        in_specs=[VM()] * 8,
         out_specs=(VM(), VM()),
         scratch_shapes=[
             pltpu.VMEM((KT + 16, POS), BF),
@@ -335,14 +335,16 @@
     own = jnp.transpose(latent_features[0], (1, 2, 0, 3))
     even = [(i, i ^ 1) for i in range(n_rows)]
     odd = [(i, ((i + 1) ^ 1) - 1) for i in range(1, n_rows - 1)]
-    pair = jnp.stack([lax.ppermute(own, EDGE_AXES, even), lax.ppermute(own, EDGE_AXES, odd)])
+    axes = EDGE_AXES + ("c",)
+    one = lax.ppermute(own, axes, [(2 * i, 2 * j) for i, j in even] + [(2 * i + 1, 2 * j + 1) for i, j in odd])
+    two = lax.ppermute(own, axes, [(2 * i, 2 * j) for i, j in odd] + [(2 * i + 1, 2 * j + 1) for i, j in even])
 
     wt = jnp.transpose(conv_weight.reshape(3, KT, C), (0, 2, 1)).reshape(3 * C, KT)
     wo = jnp.pad(jnp.transpose(out_weight, (2, 0, 1)), ((0, 0), (0, 5), (0, 0))).reshape(C, C)
     ob = jnp.pad(out_bias[:, None], ((0, 5), (0, 0)))
     tgt = jnp.pad(target_frames[0].reshape(3, F * 2 * W).astype(F32), ((0, 5), (0, 0)))
 
-    decoded, packed = k1_call(n_rows, scale)(own, pair, wt, conv_bias[:, None], wo, ob, tgt)
+    decoded, packed = k1_call(n_rows, scale)(own, one, two, wt, conv_bias[:, None], wo, ob, tgt)
 
     chunk = ROWS // near
 

time: 83.3 us -> 82.4 us (0.989)
  starting transfers between devices: 19.6 us -> 17.9 us
  blocking collectives: 43.3 us -> 44.6 us
    ppermute x2, starting transfers between devices: 7.24 us -> 4.71 us  [the longest x1 4.03 us: local(): lax.ppermute(own, axes, [(2 * i, 2 * j) for i, j in odd] + [(2 * i + 1, 2...]
    all_to_all x1, blocking collectives: 24.3 us -> 25.5 us  [local(): lax.all_to_all(packed.reshape(near, chunk, W), AXES, 0, 0, axis_index_gro...]
    ppermute x9, starting transfers between devices: 12.3 us -> 13.2 us  [pass_on(): lax.ppermute(value, DEPTH[::-1], [(place[i], place[j]) for i, j in pairs])]
where the time goes in v6:
time: 82.4 us; the launch traced here: 81.6 us
  blocking collectives  44.6 us (54%)
  starting transfers between devices  17.9 us (22%)
  waiting for transfers between devices  7.16 us (9%)
  Pallas kernels  6.42 us (8%)
  local copies, waits for them, and re-layouts  4.62 us (6%)
  between operations  0.84 us (1%)
    all_to_all x1, blocking collectives, local(): lax.all_to_all(packed.reshape(near, chunk, W), AXES, 0, 0, axis_index_gro...  25.5 us
    all_to_all x1, blocking collectives, local(): lax.all_to_all(parts, AXES, 0, 0, axis_index_groups=scatter_groups())  19.1 us
    ppermute x9, starting transfers between devices, pass_on(): lax.ppermute(value, DEPTH[::-1], [(place[i], place[j]) for i, j in pairs])  13.2 us
    ppermute x9, waiting for transfers between devices, pass_on(): lax.ppermute(value, DEPTH[::-1], [(place[i], place[j]) for i, j in pairs])  7.16 us
    pallas_call x1, Pallas kernels, local(): k1_call(n_rows, scale)(own, one, two, wt, conv_bias[:, None], wo, ob, tgt)  4.91 us
    ppermute x1, starting transfers between devices, local(): lax.ppermute(own, axes, [(2 * i, 2 * j) for i, j in odd] + [(2 * i + 1, 2...  4.03 us
  transfers between devices with their start and end apart: 11, of which 4 were waited for; matrix products, arithmetic and copies ran while one was open for 4% of the time, Pallas kernels for 0%

profile of v6, /device:TPU:1, one launch (start us, length us, event | category | flops | bytes accessed | tf_op | source)
XLA Modules:
  0.0 81.6 jit_solution(15599544708903108118)
XLA Ops:
  0.6 0.0 copy-start
  0.6 1.0 %copy.16 = bf16[1,96,5,2,128]{4,1,3,2,0:T(8,128)(2,1)S(1)} copy(bf16[1,96,5,2,128]{4,3,2,1,0:T(2,128)(2,1)} %param.6) | data formatting | bytes 491520 | tf_op args[0]
  1.6 4.0 %collective-permute-start.1 = (bf16[5,2,96,128]{3,2,1,0:T(8,128)(2,1)S(1)}, bf16[5,2,96,128]{3,2,1,0:T(8,128)(2,1)S(1)}, u32[]{:S(2)}, u32[]{:S(2)}) collective-permute-start(bf16[5,2,96,128]{3,2,1,0:T(8,128)(2,1)S(1)} %bitcast.19), channel_id=1, source_target_pairs={{8,16},{16,8},{24,32},{32,24},{40,48},{48,40},{56,64},{64,56},{72,... | collective-permute-start | bytes 737288 | tf_op jit(solution)/shard_map/ppermute | solution.py:340
  5.7 0.7 collective-permute-start
  6.4 0.7 copy.13
  7.1 0.7 convert_element_type.10
  7.8 0.8 copy.14.cb_ref
  8.6 1.4 %copy.12 = bf16[3,864,96]{1,2,0:T(8,128)(2,1)S(1)} copy(bf16[3,864,96]{2,1,0:T(8,128)(2,1)} %bitcast.24) | data formatting | bytes 995328 | tf_op jit(solution)/shard_map/reshape | solution.py:342
  10.0 0.0 copy-done
  10.0 0.0 collective-permute-done.1.two_ref
  10.0 0.0 collective-permute-done.one_ref
  10.0 4.9 %device_part.1 = (bf16[1,3,5,2,128]{4,3,2,1,0:T(2,128)(2,1)}, bf16[2048,128]{1,0:T(8,128)(2,1)S(1)}) custom-call(bf16[5,2,96,128]{3,2,1,0:T(8,128)(2,1)S(1)} %bitcast.21, bf16[5,2,96,128]{3,2,1,0:T(8,128)(2,1)S(1)} %collective-permute-done.one_ref, bf16[5,2,96,128]{3,2,1,0:T(8,128)(2,1)S(1)} %collective-permute-done.1.two_ref, ...), custom_call_target="tpu_custom_call" | custom-call | tf_op jit(solution)/shard_map/device_part/pallas_call | solution.py:347
  15.0 25.5 %all_to_all.10.in_ref = bf16[64,32,128]{2,1,0:T(8,128)(2,1)S(1)} all-to-all(bf16[64,32,128]{2,1,0:T(8,128)(2,1)S(1)} %bitcast.22), channel_id=1, replica_groups={{289,288,297,296,305,304,313,312,257,256,265,264,273,272,281,280,417,41..., dimensions={0} | all-to-all | bytes 1048576 | tf_op jit(solution)/shard_map/all_to_all | solution.py:361
  40.5 0.1 plane_sum.1.part_ref.refs_0_
  40.6 0.7 collective-permute-start.2
  41.3 1.3 %collective-permute-start.7 = (bf16[32,128]{1,0:T(8,128)(2,1)S(1)}, bf16[32,128]{1,0:T(8,128)(2,1)S(1)}, u32[]{:S(2)}, u32[]{:S(2)}) collective-permute-start(bf16[32,128]{1,0:T(8,128)(2,1)S(1)} %plane_sum.1.part_ref.refs_0_), channel_id=1, source_target_pairs={{68,0},{4,64},{69,1},{5,65},{76,8},{12,72},{77,9},{13,73},{84,16},... | collective-permute-start | bytes 24584 | tf_op jit(solution)/shard_map/ppermute | solution.py:247
  42.6 1.3 %collective-permute-start.6 = (bf16[32,128]{1,0:T(8,128)(2,1)S(1)}, bf16[32,128]{1,0:T(8,128)(2,1)S(1)}, u32[]{:S(2)}, u32[]{:S(2)}) collective-permute-start(bf16[32,128]{1,0:T(8,128)(2,1)S(1)} %plane_sum.1.part_ref.refs_0_), channel_id=1, source_target_pairs={{4,0},{68,64},{5,1},{69,65},{12,8},{76,72},{13,9},{77,73},{20,16},... | collective-permute-start | bytes 24584 | tf_op jit(solution)/shard_map/ppermute | solution.py:247
  43.9 0.0 collective-permute-done.2.side_ref
  43.9 1.3 %collective-permute-start.5 = (bf16[32,128]{1,0:T(8,128)(2,1)S(1)}, bf16[32,128]{1,0:T(8,128)(2,1)S(1)}, u32[]{:S(2)}, u32[]{:S(2)}) collective-permute-start(bf16[32,128]{1,0:T(8,128)(2,1)S(1)} %side_sum.1), channel_id=1, source_target_pairs={{6,64},{2,0},{7,65},{3,1},{14,72},{10,8},{15,73},{11,9},{22,80},{1... | collective-permute-start | bytes 24584 | tf_op jit(solution)/shard_map/ppermute | solution.py:247
  45.2 1.3 %collective-permute-start.4 = (bf16[32,128]{1,0:T(8,128)(2,1)S(1)}, bf16[32,128]{1,0:T(8,128)(2,1)S(1)}, u32[]{:S(2)}, u32[]{:S(2)}) collective-permute-start(bf16[32,128]{1,0:T(8,128)(2,1)S(1)} %side_sum.1), channel_id=1, source_target_pairs={{6,0},{2,64},{7,1},{3,65},{14,8},{10,72},{15,9},{11,73},{22,16},{1... | collective-permute-start | bytes 24584 | tf_op jit(solution)/shard_map/ppermute | solution.py:247
  46.5 4.8 %collective-permute-start.3 = (bf16[32,128]{1,0:T(8,128)(2,1)S(1)}, bf16[32,128]{1,0:T(8,128)(2,1)S(1)}, u32[]{:S(2)}, u32[]{:S(2)}) collective-permute-start(bf16[32,128]{1,0:T(8,128)(2,1)S(1)} %side_sum.1), channel_id=1, source_target_pairs={{64,0},{0,64},{65,1},{1,65},{72,8},{8,72},{73,9},{9,73},{80,16},{1... | collective-permute-start | bytes 24584 | tf_op jit(solution)/shard_map/ppermute | solution.py:247
  51.3 3.9 %collective-permute-done.7.refs_5_ = bf16[32,128]{1,0:T(8,128)(2,1)S(1)} collective-permute-done((bf16[32,128]{1,0:T(8,128)(2,1)S(1)}, bf16[32,128]{1,0:T(8,128)(2,1)S(1)}, u32[]{:S(2)}, u32[]{:S(2)}) %collective-permute-start.7) | collective-permute-done | bytes 8224 | tf_op jit(solution)/shard_map/ppermute | solution.py:247
  55.2 1.3 %collective-permute-done.6.refs_4_ = bf16[32,128]{1,0:T(8,128)(2,1)S(1)} collective-permute-done((bf16[32,128]{1,0:T(8,128)(2,1)S(1)}, bf16[32,128]{1,0:T(8,128)(2,1)S(1)}, u32[]{:S(2)}, u32[]{:S(2)}) %collective-permute-start.6) | collective-permute-done | bytes 8224 | tf_op jit(solution)/shard_map/ppermute | solution.py:247
  56.5 0.0 collective-permute-done.5.refs_3_
  56.5 1.2 %collective-permute-done.4.refs_2_ = bf16[32,128]{1,0:T(8,128)(2,1)S(1)} collective-permute-done((bf16[32,128]{1,0:T(8,128)(2,1)S(1)}, bf16[32,128]{1,0:T(8,128)(2,1)S(1)}, u32[]{:S(2)}, u32[]{:S(2)}) %collective-permute-start.4) | collective-permute-done | bytes 8224 | tf_op jit(solution)/shard_map/ppermute | solution.py:247
  57.7 0.0 collective-permute-done.3.refs_1_
  57.7 1.3 %collective-permute-start.8 = (bf16[32,128]{1,0:T(8,128)(2,1)S(1)}, bf16[32,128]{1,0:T(8,128)(2,1)S(1)}, u32[]{:S(2)}, u32[]{:S(2)}) collective-permute-start(bf16[32,128]{1,0:T(8,128)(2,1)S(1)} %depth_sum.1), channel_id=1, source_target_pairs={{0,2},{64,66},{1,3},{65,67},{8,10},{72,74},{9,11},{73,75},{16,18},... | collective-permute-start | bytes 24584 | tf_op jit(solution)/shard_map/ppermute | solution.py:247
  59.0 0.8 collective-permute-done.8
  59.8 0.6 collective-permute-start.9
  60.4 0.0 collective-permute-done.9
  60.5 0.7 collective-permute-start.10
  61.1 0.0 collective-permute-done.10.two_ref
  61.2 19.1 %all_to_all.11 = bf16[64,32,128]{2,1,0:T(8,128)(2,1)S(1)} all-to-all(bf16[64,32,128]{2,1,0:T(8,128)(2,1)S(1)} %copies.1), channel_id=1, replica_groups={{289,288,297,296,305,304,313,312,257,256,265,264,273,272,281,280,417,41..., dimensions={0} | all-to-all | bytes 1048576 | tf_op jit(solution)/shard_map/all_to_all | solution.py:372
  80.2 1.3 %unpack.1 = (f32[2592,96]{1,0:T(8,128)}, f32[96]{0:T(128)}, f32[3,27,96]{2,1,0:T(8,128)}, f32[3]{0:T(128)}) custom-call(bf16[2048,128]{1,0:T(8,128)(2,1)S(1)} %bitcast.17), custom_call_target="tpu_custom_call" | custom-call | tf_op jit(solution)/shard_map/unpack/pallas_call | solution.py:374
  (8 shorter events, 0.1 us)
Async XLA Ops:
  0.6 9.4 %copy-start = (bf16[27,96,3]{1,0,2:T(8,128)(2,1)S(1)}, bf16[27,96,3]{1,0,2:T(8,128)(2,1)}, u32[]{:S(2)}) copy-start(bf16[27,96,3]{1,0,2:T(8,128)(2,1)} %param.9) | copy-start | bytes 46660
  1.6 8.4 %collective-permute-start.1 = (bf16[5,2,96,128]{3,2,1,0:T(8,128)(2,1)S(1)}, bf16[5,2,96,128]{3,2,1,0:T(8,128)(2,1)S(1)}, u32[]{:S(2)}, u32[]{:S(2)}) collective-permute-start(bf16[5,2,96,128]{3,2,1,0:T(8,128)(2,1)S(1)} %bitcast.19), channel_id=1, source_target_pairs={{8,16},{16,8},{24,32},{32,24},{40,48},{48,40},{56,64},{64,56},{72,... | collective-permute-start | bytes 737288 | tf_op jit(solution)/shard_map/ppermute | solution.py:340
  5.7 4.4 %collective-permute-start = (bf16[5,2,96,128]{3,2,1,0:T(8,128)(2,1)S(1)}, bf16[5,2,96,128]{3,2,1,0:T(8,128)(2,1)S(1)}, u32[]{:S(2)}, u32[]{:S(2)}) collective-permute-start(bf16[5,2,96,128]{3,2,1,0:T(8,128)(2,1)S(1)} %bitcast.20), channel_id=1, source_target_pairs={{0,8},{8,0},{16,24},{24,16},{32,40},{40,32},{48,56},{56,48},{64,72... | collective-permute-start | bytes 737288 | tf_op jit(solution)/shard_map/ppermute | solution.py:339
  40.6 3.3 %collective-permute-start.2 = (bf16[32,128]{1,0:T(8,128)(2,1)S(1)}, bf16[32,128]{1,0:T(8,128)(2,1)S(1)}, u32[]{:S(2)}, u32[]{:S(2)}) collective-permute-start(bf16[32,128]{1,0:T(8,128)(2,1)S(1)} %plane_sum.1.part_ref.refs_0_), channel_id=1, source_target_pairs={{70,6},{66,2},{71,7},{67,3},{78,14},{74,10},{79,15},{75,11},{86,22... | collective-permute-start | bytes 24584 | tf_op jit(solution)/shard_map/ppermute | solution.py:247
  41.3 13.9 %collective-permute-start.7 = (bf16[32,128]{1,0:T(8,128)(2,1)S(1)}, bf16[32,128]{1,0:T(8,128)(2,1)S(1)}, u32[]{:S(2)}, u32[]{:S(2)}) collective-permute-start(bf16[32,128]{1,0:T(8,128)(2,1)S(1)} %plane_sum.1.part_ref.refs_0_), channel_id=1, source_target_pairs={{68,0},{4,64},{69,1},{5,65},{76,8},{12,72},{77,9},{13,73},{84,16},... | collective-permute-start | bytes 24584 | tf_op jit(solution)/shard_map/ppermute | solution.py:247
  42.6 13.9 %collective-permute-start.6 = (bf16[32,128]{1,0:T(8,128)(2,1)S(1)}, bf16[32,128]{1,0:T(8,128)(2,1)S(1)}, u32[]{:S(2)}, u32[]{:S(2)}) collective-permute-start(bf16[32,128]{1,0:T(8,128)(2,1)S(1)} %plane_sum.1.part_ref.refs_0_), channel_id=1, source_target_pairs={{4,0},{68,64},{5,1},{69,65},{12,8},{76,72},{13,9},{77,73},{20,16},... | collective-permute-start | bytes 24584 | tf_op jit(solution)/shard_map/ppermute | solution.py:247
  43.9 12.6 %collective-permute-start.5 = (bf16[32,128]{1,0:T(8,128)(2,1)S(1)}, bf16[32,128]{1,0:T(8,128)(2,1)S(1)}, u32[]{:S(2)}, u32[]{:S(2)}) collective-permute-start(bf16[32,128]{1,0:T(8,128)(2,1)S(1)} %side_sum.1), channel_id=1, source_target_pairs={{6,64},{2,0},{7,65},{3,1},{14,72},{10,8},{15,73},{11,9},{22,80},{1... | collective-permute-start | bytes 24584 | tf_op jit(solution)/shard_map/ppermute | solution.py:247
  45.2 12.5 %collective-permute-start.4 = (bf16[32,128]{1,0:T(8,128)(2,1)S(1)}, bf16[32,128]{1,0:T(8,128)(2,1)S(1)}, u32[]{:S(2)}, u32[]{:S(2)}) collective-permute-start(bf16[32,128]{1,0:T(8,128)(2,1)S(1)} %side_sum.1), channel_id=1, source_target_pairs={{6,0},{2,64},{7,1},{3,65},{14,8},{10,72},{15,9},{11,73},{22,16},{1... | collective-permute-start | bytes 24584 | tf_op jit(solution)/shard_map/ppermute | solution.py:247
  46.5 11.2 %collective-permute-start.3 = (bf16[32,128]{1,0:T(8,128)(2,1)S(1)}, bf16[32,128]{1,0:T(8,128)(2,1)S(1)}, u32[]{:S(2)}, u32[]{:S(2)}) collective-permute-start(bf16[32,128]{1,0:T(8,128)(2,1)S(1)} %side_sum.1), channel_id=1, source_target_pairs={{64,0},{0,64},{65,1},{1,65},{72,8},{8,72},{73,9},{9,73},{80,16},{1... | collective-permute-start | bytes 24584 | tf_op jit(solution)/shard_map/ppermute | solution.py:247
  57.7 2.1 %collective-permute-start.8 = (bf16[32,128]{1,0:T(8,128)(2,1)S(1)}, bf16[32,128]{1,0:T(8,128)(2,1)S(1)}, u32[]{:S(2)}, u32[]{:S(2)}) collective-permute-start(bf16[32,128]{1,0:T(8,128)(2,1)S(1)} %depth_sum.1), channel_id=1, source_target_pairs={{0,2},{64,66},{1,3},{65,67},{8,10},{72,74},{9,11},{73,75},{16,18},... | collective-permute-start | bytes 24584 | tf_op jit(solution)/shard_map/ppermute | solution.py:247
  59.8 0.7 collective-permute-start.9
  60.5 0.7 collective-permute-start.10

commit v7 on v6

--- a/solution.py
+++ b/solution.py
@@ -32,7 +32,7 @@
 FAR = (((5, 0), (4, 1)), ((4, 0), (5, 1)))
 SIDE = ((7, 6), (3, 2))
 CLOSE = (((6, 1), (2, 0)), ((6, 0), (2, 1)), ((1, 0), (0, 1)))
-SPREAD = (((0, 2), (1, 3)), ((1, 7), (3, 5)), ((2, 4), (7, 6)))
+SPREAD = (((0, 2), (1, 3)), ((1, 7),), ((2, 4), (3, 5), (7, 6)))
 
 
 def nt(a, b):
@@ -365,8 +365,8 @@
     close = [pass_on(more, pairs) for pairs in CLOSE[::-1]]
     far = [pass_on(part, pairs) for pairs in FAR[::-1]]
     total = small(depth_sum_kernel, "depth_sum", (), part, *close, *far)
-    for pairs in SPREAD[:-1]:
-        total = total + pass_on(total, pairs)
+    received = [pass_on(total, pairs) for pairs in SPREAD[:-1]]
+    total = sum(received, total)
     outer = pass_on(total, SPREAD[-1])
     parts = small(copies_kernel, "copies", (near,), total, outer)
     parts = lax.all_to_all(parts, AXES, 0, 0, axis_index_groups=scatter_groups())

time: 82.4 us -> 82.2 us (level)
  no operation moved by 1% of the time
where the time goes in v7:
time: 82.2 us; the launch traced here: 81.5 us
  blocking collectives  44.6 us (54%)
  starting transfers between devices  17.9 us (22%)
  waiting for transfers between devices  7.15 us (9%)
  Pallas kernels  6.42 us (8%)
  local copies, waits for them, and re-layouts  4.62 us (6%)
  between operations  0.83 us (1%)
    all_to_all x1, blocking collectives, local(): lax.all_to_all(packed.reshape(near, chunk, W), AXES, 0, 0, axis_index_gro...  25.5 us
    all_to_all x1, blocking collectives, local(): lax.all_to_all(parts, AXES, 0, 0, axis_index_groups=scatter_groups())  19.1 us
    ppermute x9, starting transfers between devices, pass_on(): lax.ppermute(value, DEPTH[::-1], [(place[i], place[j]) for i, j in pairs])  13.2 us
    ppermute x9, waiting for transfers between devices, pass_on(): lax.ppermute(value, DEPTH[::-1], [(place[i], place[j]) for i, j in pairs])  7.15 us
    pallas_call x1, Pallas kernels, local(): k1_call(n_rows, scale)(own, one, two, wt, conv_bias[:, None], wo, ob, tgt)  4.91 us
    ppermute x1, starting transfers between devices, local(): lax.ppermute(own, axes, [(2 * i, 2 * j) for i, j in odd] + [(2 * i + 1, 2...  4.03 us
  transfers between devices with their start and end apart: 11, of which 4 were waited for; matrix products, arithmetic and copies ran while one was open for 4% of the time, Pallas kernels for 0%

profile of v7, /device:TPU:1, one launch (start us, length us, event | category | flops | bytes accessed | tf_op | source)
XLA Modules:
  0.0 81.5 jit_solution(15925176608935660222)
XLA Ops:
  0.6 0.0 copy-start
  0.6 1.0 %copy.16 = bf16[1,96,5,2,128]{4,1,3,2,0:T(8,128)(2,1)S(1)} copy(bf16[1,96,5,2,128]{4,3,2,1,0:T(2,128)(2,1)} %param.6) | data formatting | bytes 491520 | tf_op args[0]
  1.6 4.0 %collective-permute-start.1 = (bf16[5,2,96,128]{3,2,1,0:T(8,128)(2,1)S(1)}, bf16[5,2,96,128]{3,2,1,0:T(8,128)(2,1)S(1)}, u32[]{:S(2)}, u32[]{:S(2)}) collective-permute-start(bf16[5,2,96,128]{3,2,1,0:T(8,128)(2,1)S(1)} %bitcast.19), channel_id=1, source_target_pairs={{8,16},{16,8},{24,32},{32,24},{40,48},{48,40},{56,64},{64,56},{72,... | collective-permute-start | bytes 737288 | tf_op jit(solution)/shard_map/ppermute | solution.py:340
  5.7 0.7 collective-permute-start
  6.4 0.7 copy.13
  7.1 0.7 convert_element_type.10
  7.8 0.8 copy.14.cb_ref
  8.6 1.4 %copy.12 = bf16[3,864,96]{1,2,0:T(8,128)(2,1)S(1)} copy(bf16[3,864,96]{2,1,0:T(8,128)(2,1)} %bitcast.24) | data formatting | bytes 995328 | tf_op jit(solution)/shard_map/reshape | solution.py:342
  10.0 0.0 copy-done
  10.0 0.0 collective-permute-done.1.two_ref
  10.0 0.0 collective-permute-done.one_ref
  10.0 4.9 %device_part.1 = (bf16[1,3,5,2,128]{4,3,2,1,0:T(2,128)(2,1)}, bf16[2048,128]{1,0:T(8,128)(2,1)S(1)}) custom-call(bf16[5,2,96,128]{3,2,1,0:T(8,128)(2,1)S(1)} %bitcast.21, bf16[5,2,96,128]{3,2,1,0:T(8,128)(2,1)S(1)} %collective-permute-done.one_ref, bf16[5,2,96,128]{3,2,1,0:T(8,128)(2,1)S(1)} %collective-permute-done.1.two_ref, ...), custom_call_target="tpu_custom_call" | custom-call | tf_op jit(solution)/shard_map/device_part/pallas_call | solution.py:347
  15.0 25.5 %all_to_all.10.in_ref = bf16[64,32,128]{2,1,0:T(8,128)(2,1)S(1)} all-to-all(bf16[64,32,128]{2,1,0:T(8,128)(2,1)S(1)} %bitcast.22), channel_id=1, replica_groups={{289,288,297,296,305,304,313,312,257,256,265,264,273,272,281,280,417,41..., dimensions={0} | all-to-all | bytes 1048576 | tf_op jit(solution)/shard_map/all_to_all | solution.py:361
  40.5 0.1 plane_sum.1.part_ref.refs_0_
  40.6 0.7 collective-permute-start.2
  41.3 1.3 %collective-permute-start.7 = (bf16[32,128]{1,0:T(8,128)(2,1)S(1)}, bf16[32,128]{1,0:T(8,128)(2,1)S(1)}, u32[]{:S(2)}, u32[]{:S(2)}) collective-permute-start(bf16[32,128]{1,0:T(8,128)(2,1)S(1)} %plane_sum.1.part_ref.refs_0_), channel_id=1, source_target_pairs={{68,0},{4,64},{69,1},{5,65},{76,8},{12,72},{77,9},{13,73},{84,16},... | collective-permute-start | bytes 24584 | tf_op jit(solution)/shard_map/ppermute | solution.py:247
  42.6 1.3 %collective-permute-start.6 = (bf16[32,128]{1,0:T(8,128)(2,1)S(1)}, bf16[32,128]{1,0:T(8,128)(2,1)S(1)}, u32[]{:S(2)}, u32[]{:S(2)}) collective-permute-start(bf16[32,128]{1,0:T(8,128)(2,1)S(1)} %plane_sum.1.part_ref.refs_0_), channel_id=1, source_target_pairs={{4,0},{68,64},{5,1},{69,65},{12,8},{76,72},{13,9},{77,73},{20,16},... | collective-permute-start | bytes 24584 | tf_op jit(solution)/shard_map/ppermute | solution.py:247
  43.9 0.0 collective-permute-done.2.side_ref
  43.9 1.3 %collective-permute-start.5 = (bf16[32,128]{1,0:T(8,128)(2,1)S(1)}, bf16[32,128]{1,0:T(8,128)(2,1)S(1)}, u32[]{:S(2)}, u32[]{:S(2)}) collective-permute-start(bf16[32,128]{1,0:T(8,128)(2,1)S(1)} %side_sum.1), channel_id=1, source_target_pairs={{6,64},{2,0},{7,65},{3,1},{14,72},{10,8},{15,73},{11,9},{22,80},{1... | collective-permute-start | bytes 24584 | tf_op jit(solution)/shard_map/ppermute | solution.py:247
  45.2 1.3 %collective-permute-start.4 = (bf16[32,128]{1,0:T(8,128)(2,1)S(1)}, bf16[32,128]{1,0:T(8,128)(2,1)S(1)}, u32[]{:S(2)}, u32[]{:S(2)}) collective-permute-start(bf16[32,128]{1,0:T(8,128)(2,1)S(1)} %side_sum.1), channel_id=1, source_target_pairs={{6,0},{2,64},{7,1},{3,65},{14,8},{10,72},{15,9},{11,73},{22,16},{1... | collective-permute-start | bytes 24584 | tf_op jit(solution)/shard_map/ppermute | solution.py:247
  46.5 4.8 %collective-permute-start.3 = (bf16[32,128]{1,0:T(8,128)(2,1)S(1)}, bf16[32,128]{1,0:T(8,128)(2,1)S(1)}, u32[]{:S(2)}, u32[]{:S(2)}) collective-permute-start(bf16[32,128]{1,0:T(8,128)(2,1)S(1)} %side_sum.1), channel_id=1, source_target_pairs={{64,0},{0,64},{65,1},{1,65},{72,8},{8,72},{73,9},{9,73},{80,16},{1... | collective-permute-start | bytes 24584 | tf_op jit(solution)/shard_map/ppermute | solution.py:247
  51.3 3.9 %collective-permute-done.7.refs_5_ = bf16[32,128]{1,0:T(8,128)(2,1)S(1)} collective-permute-done((bf16[32,128]{1,0:T(8,128)(2,1)S(1)}, bf16[32,128]{1,0:T(8,128)(2,1)S(1)}, u32[]{:S(2)}, u32[]{:S(2)}) %collective-permute-start.7) | collective-permute-done | bytes 8224 | tf_op jit(solution)/shard_map/ppermute | solution.py:247
  55.2 1.3 %collective-permute-done.6.refs_4_ = bf16[32,128]{1,0:T(8,128)(2,1)S(1)} collective-permute-done((bf16[32,128]{1,0:T(8,128)(2,1)S(1)}, bf16[32,128]{1,0:T(8,128)(2,1)S(1)}, u32[]{:S(2)}, u32[]{:S(2)}) %collective-permute-start.6) | collective-permute-done | bytes 8224 | tf_op jit(solution)/shard_map/ppermute | solution.py:247
  56.5 0.0 collective-permute-done.5.refs_3_
  56.5 1.2 %collective-permute-done.4.refs_2_ = bf16[32,128]{1,0:T(8,128)(2,1)S(1)} collective-permute-done((bf16[32,128]{1,0:T(8,128)(2,1)S(1)}, bf16[32,128]{1,0:T(8,128)(2,1)S(1)}, u32[]{:S(2)}, u32[]{:S(2)}) %collective-permute-start.4) | collective-permute-done | bytes 8224 | tf_op jit(solution)/shard_map/ppermute | solution.py:247
  57.7 0.0 collective-permute-done.3.refs_1_
  57.7 0.7 collective-permute-start.9
  58.4 1.3 %collective-permute-start.8 = (bf16[32,128]{1,0:T(8,128)(2,1)S(1)}, bf16[32,128]{1,0:T(8,128)(2,1)S(1)}, u32[]{:S(2)}, u32[]{:S(2)}) collective-permute-start(bf16[32,128]{1,0:T(8,128)(2,1)S(1)} %depth_sum.1), channel_id=1, source_target_pairs={{0,2},{64,66},{1,3},{65,67},{8,10},{72,74},{9,11},{73,75},{16,18},... | collective-permute-start | bytes 24584 | tf_op jit(solution)/shard_map/ppermute | solution.py:247
  59.7 0.0 collective-permute-done.9
  59.7 0.8 collective-permute-done.8
  60.5 0.6 collective-permute-start.10
  61.1 0.0 collective-permute-done.10.two_ref
  61.2 19.1 %all_to_all.11 = bf16[64,32,128]{2,1,0:T(8,128)(2,1)S(1)} all-to-all(bf16[64,32,128]{2,1,0:T(8,128)(2,1)S(1)} %copies.1), channel_id=1, replica_groups={{289,288,297,296,305,304,313,312,257,256,265,264,273,272,281,280,417,41..., dimensions={0} | all-to-all | bytes 1048576 | tf_op jit(solution)/shard_map/all_to_all | solution.py:372
  80.2 1.3 %unpack.1 = (f32[2592,96]{1,0:T(8,128)}, f32[96]{0:T(128)}, f32[3,27,96]{2,1,0:T(8,128)}, f32[3]{0:T(128)}) custom-call(bf16[2048,128]{1,0:T(8,128)(2,1)S(1)} %bitcast.17), custom_call_target="tpu_custom_call" | custom-call | tf_op jit(solution)/shard_map/unpack/pallas_call | solution.py:374
  (7 shorter events, 0.1 us)
Async XLA Ops:
  0.6 9.4 %copy-start = (bf16[27,96,3]{1,0,2:T(8,128)(2,1)S(1)}, bf16[27,96,3]{1,0,2:T(8,128)(2,1)}, u32[]{:S(2)}) copy-start(bf16[27,96,3]{1,0,2:T(8,128)(2,1)} %param.9) | copy-start | bytes 46660
  1.6 8.4 %collective-permute-start.1 = (bf16[5,2,96,128]{3,2,1,0:T(8,128)(2,1)S(1)}, bf16[5,2,96,128]{3,2,1,0:T(8,128)(2,1)S(1)}, u32[]{:S(2)}, u32[]{:S(2)}) collective-permute-start(bf16[5,2,96,128]{3,2,1,0:T(8,128)(2,1)S(1)} %bitcast.19), channel_id=1, source_target_pairs={{8,16},{16,8},{24,32},{32,24},{40,48},{48,40},{56,64},{64,56},{72,... | collective-permute-start | bytes 737288 | tf_op jit(solution)/shard_map/ppermute | solution.py:340
  5.7 4.4 %collective-permute-start = (bf16[5,2,96,128]{3,2,1,0:T(8,128)(2,1)S(1)}, bf16[5,2,96,128]{3,2,1,0:T(8,128)(2,1)S(1)}, u32[]{:S(2)}, u32[]{:S(2)}) collective-permute-start(bf16[5,2,96,128]{3,2,1,0:T(8,128)(2,1)S(1)} %bitcast.20), channel_id=1, source_target_pairs={{0,8},{8,0},{16,24},{24,16},{32,40},{40,32},{48,56},{56,48},{64,72... | collective-permute-start | bytes 737288 | tf_op jit(solution)/shard_map/ppermute | solution.py:339
  40.6 3.3 %collective-permute-start.2 = (bf16[32,128]{1,0:T(8,128)(2,1)S(1)}, bf16[32,128]{1,0:T(8,128)(2,1)S(1)}, u32[]{:S(2)}, u32[]{:S(2)}) collective-permute-start(bf16[32,128]{1,0:T(8,128)(2,1)S(1)} %plane_sum.1.part_ref.refs_0_), channel_id=1, source_target_pairs={{70,6},{66,2},{71,7},{67,3},{78,14},{74,10},{79,15},{75,11},{86,22... | collective-permute-start | bytes 24584 | tf_op jit(solution)/shard_map/ppermute | solution.py:247
  41.3 13.9 %collective-permute-start.7 = (bf16[32,128]{1,0:T(8,128)(2,1)S(1)}, bf16[32,128]{1,0:T(8,128)(2,1)S(1)}, u32[]{:S(2)}, u32[]{:S(2)}) collective-permute-start(bf16[32,128]{1,0:T(8,128)(2,1)S(1)} %plane_sum.1.part_ref.refs_0_), channel_id=1, source_target_pairs={{68,0},{4,64},{69,1},{5,65},{76,8},{12,72},{77,9},{13,73},{84,16},... | collective-permute-start | bytes 24584 | tf_op jit(solution)/shard_map/ppermute | solution.py:247
  42.6 13.9 %collective-permute-start.6 = (bf16[32,128]{1,0:T(8,128)(2,1)S(1)}, bf16[32,128]{1,0:T(8,128)(2,1)S(1)}, u32[]{:S(2)}, u32[]{:S(2)}) collective-permute-start(bf16[32,128]{1,0:T(8,128)(2,1)S(1)} %plane_sum.1.part_ref.refs_0_), channel_id=1, source_target_pairs={{4,0},{68,64},{5,1},{69,65},{12,8},{76,72},{13,9},{77,73},{20,16},... | collective-permute-start | bytes 24584 | tf_op jit(solution)/shard_map/ppermute | solution.py:247
  43.9 12.6 %collective-permute-start.5 = (bf16[32,128]{1,0:T(8,128)(2,1)S(1)}, bf16[32,128]{1,0:T(8,128)(2,1)S(1)}, u32[]{:S(2)}, u32[]{:S(2)}) collective-permute-start(bf16[32,128]{1,0:T(8,128)(2,1)S(1)} %side_sum.1), channel_id=1, source_target_pairs={{6,64},{2,0},{7,65},{3,1},{14,72},{10,8},{15,73},{11,9},{22,80},{1... | collective-permute-start | bytes 24584 | tf_op jit(solution)/shard_map/ppermute | solution.py:247
  45.2 12.5 %collective-permute-start.4 = (bf16[32,128]{1,0:T(8,128)(2,1)S(1)}, bf16[32,128]{1,0:T(8,128)(2,1)S(1)}, u32[]{:S(2)}, u32[]{:S(2)}) collective-permute-start(bf16[32,128]{1,0:T(8,128)(2,1)S(1)} %side_sum.1), channel_id=1, source_target_pairs={{6,0},{2,64},{7,1},{3,65},{14,8},{10,72},{15,9},{11,73},{22,16},{1... | collective-permute-start | bytes 24584 | tf_op jit(solution)/shard_map/ppermute | solution.py:247
  46.5 11.2 %collective-permute-start.3 = (bf16[32,128]{1,0:T(8,128)(2,1)S(1)}, bf16[32,128]{1,0:T(8,128)(2,1)S(1)}, u32[]{:S(2)}, u32[]{:S(2)}) collective-permute-start(bf16[32,128]{1,0:T(8,128)(2,1)S(1)} %side_sum.1), channel_id=1, source_target_pairs={{64,0},{0,64},{65,1},{1,65},{72,8},{8,72},{73,9},{9,73},{80,16},{1... | collective-permute-start | bytes 24584 | tf_op jit(solution)/shard_map/ppermute | solution.py:247
  57.7 2.0 %collective-permute-start.9 = (bf16[32,128]{1,0:T(8,128)(2,1)S(1)}, bf16[32,128]{1,0:T(8,128)(2,1)S(1)}, u32[]{:S(2)}, u32[]{:S(2)}) collective-permute-start(bf16[32,128]{1,0:T(8,128)(2,1)S(1)} %depth_sum.1), channel_id=1, source_target_pairs={{64,70},{65,71},{72,78},{73,79},{80,86},{81,87},{88,94},{89,95},{9... | collective-permute-start | bytes 24584 | tf_op jit(solution)/shard_map/ppermute | solution.py:247
  58.4 2.1 %collective-permute-start.8 = (bf16[32,128]{1,0:T(8,128)(2,1)S(1)}, bf16[32,128]{1,0:T(8,128)(2,1)S(1)}, u32[]{:S(2)}, u32[]{:S(2)}) collective-permute-start(bf16[32,128]{1,0:T(8,128)(2,1)S(1)} %depth_sum.1), channel_id=1, source_target_pairs={{0,2},{64,66},{1,3},{65,67},{8,10},{72,74},{9,11},{73,75},{16,18},... | collective-permute-start | bytes 24584 | tf_op jit(solution)/shard_map/ppermute | solution.py:247
  60.5 0.7 collective-permute-start.10

commit v8 on v7

--- a/solution.py
+++ b/solution.py
@@ -32,7 +32,7 @@
 FAR = (((5, 0), (4, 1)), ((4, 0), (5, 1)))
 SIDE = ((7, 6), (3, 2))
 CLOSE = (((6, 1), (2, 0)), ((6, 0), (2, 1)), ((1, 0), (0, 1)))
-SPREAD = (((0, 2), (1, 3)), ((1, 7),), ((2, 4), (3, 5), (7, 6)))
+SPREAD = (((1, 7),), ((0, 2), (1, 3)), ((2, 4), (3, 5), (7, 6)))
 
 
 def nt(a, b):

time: 82.2 us -> 81.6 us (level)
  no operation moved by 1% of the time
where the time goes in v8:
time: 81.6 us; the launch traced here: 80.9 us
  blocking collectives  44.6 us (55%)
  starting transfers between devices  17.9 us (22%)
  waiting for transfers between devices  6.49 us (8%)
  Pallas kernels  6.42 us (8%)
  local copies, waits for them, and re-layouts  4.62 us (6%)
  between operations  0.83 us (1%)
    all_to_all x1, blocking collectives, local(): lax.all_to_all(packed.reshape(near, chunk, W), AXES, 0, 0, axis_index_gro...  25.5 us
    all_to_all x1, blocking collectives, local(): lax.all_to_all(parts, AXES, 0, 0, axis_index_groups=scatter_groups())  19.1 us
    ppermute x9, starting transfers between devices, pass_on(): lax.ppermute(value, DEPTH[::-1], [(place[i], place[j]) for i, j in pairs])  13.2 us
    ppermute x9, waiting for transfers between devices, pass_on(): lax.ppermute(value, DEPTH[::-1], [(place[i], place[j]) for i, j in pairs])  6.49 us
    pallas_call x1, Pallas kernels, local(): k1_call(n_rows, scale)(own, one, two, wt, conv_bias[:, None], wo, ob, tgt)  4.91 us
    ppermute x1, starting transfers between devices, local(): lax.ppermute(own, axes, [(2 * i, 2 * j) for i, j in odd] + [(2 * i + 1, 2...  4.03 us
  transfers between devices with their start and end apart: 11, of which 4 were waited for; matrix products, arithmetic and copies ran while one was open for 4% of the time, Pallas kernels for 0%

profile of v8, /device:TPU:1, one launch (start us, length us, event | category | flops | bytes accessed | tf_op | source)
XLA Modules:
  0.0 80.9 jit_solution(7711569620322969109)
XLA Ops:
  0.6 0.0 copy-start
  0.6 1.0 %copy.16 = bf16[1,96,5,2,128]{4,1,3,2,0:T(8,128)(2,1)S(1)} copy(bf16[1,96,5,2,128]{4,3,2,1,0:T(2,128)(2,1)} %param.6) | data formatting | bytes 491520 | tf_op args[0]
  1.6 4.0 %collective-permute-start.1 = (bf16[5,2,96,128]{3,2,1,0:T(8,128)(2,1)S(1)}, bf16[5,2,96,128]{3,2,1,0:T(8,128)(2,1)S(1)}, u32[]{:S(2)}, u32[]{:S(2)}) collective-permute-start(bf16[5,2,96,128]{3,2,1,0:T(8,128)(2,1)S(1)} %bitcast.19), channel_id=1, source_target_pairs={{8,16},{16,8},{24,32},{32,24},{40,48},{48,40},{56,64},{64,56},{72,... | collective-permute-start | bytes 737288 | tf_op jit(solution)/shard_map/ppermute | solution.py:340
  5.7 0.7 collective-permute-start
  6.4 0.7 copy.13
  7.1 0.7 convert_element_type.10
  7.8 0.8 copy.14.cb_ref
  8.6 1.4 %copy.12 = bf16[3,864,96]{1,2,0:T(8,128)(2,1)S(1)} copy(bf16[3,864,96]{2,1,0:T(8,128)(2,1)} %bitcast.24) | data formatting | bytes 995328 | tf_op jit(solution)/shard_map/reshape | solution.py:342
  10.0 0.0 copy-done
  10.0 0.0 collective-permute-done.1.two_ref
  10.0 0.0 collective-permute-done.one_ref
  10.0 4.9 %device_part.1 = (bf16[1,3,5,2,128]{4,3,2,1,0:T(2,128)(2,1)}, bf16[2048,128]{1,0:T(8,128)(2,1)S(1)}) custom-call(bf16[5,2,96,128]{3,2,1,0:T(8,128)(2,1)S(1)} %bitcast.21, bf16[5,2,96,128]{3,2,1,0:T(8,128)(2,1)S(1)} %collective-permute-done.one_ref, bf16[5,2,96,128]{3,2,1,0:T(8,128)(2,1)S(1)} %collective-permute-done.1.two_ref, ...), custom_call_target="tpu_custom_call" | custom-call | tf_op jit(solution)/shard_map/device_part/pallas_call | solution.py:347
  15.0 25.5 %all_to_all.10.in_ref = bf16[64,32,128]{2,1,0:T(8,128)(2,1)S(1)} all-to-all(bf16[64,32,128]{2,1,0:T(8,128)(2,1)S(1)} %bitcast.22), channel_id=1, replica_groups={{289,288,297,296,305,304,313,312,257,256,265,264,273,272,281,280,417,41..., dimensions={0} | all-to-all | bytes 1048576 | tf_op jit(solution)/shard_map/all_to_all | solution.py:361
  40.5 0.1 plane_sum.1.part_ref.refs_0_
  40.6 0.7 collective-permute-start.2
  41.3 1.3 %collective-permute-start.7 = (bf16[32,128]{1,0:T(8,128)(2,1)S(1)}, bf16[32,128]{1,0:T(8,128)(2,1)S(1)}, u32[]{:S(2)}, u32[]{:S(2)}) collective-permute-start(bf16[32,128]{1,0:T(8,128)(2,1)S(1)} %plane_sum.1.part_ref.refs_0_), channel_id=1, source_target_pairs={{68,0},{4,64},{69,1},{5,65},{76,8},{12,72},{77,9},{13,73},{84,16},... | collective-permute-start | bytes 24584 | tf_op jit(solution)/shard_map/ppermute | solution.py:247
  42.6 1.3 %collective-permute-start.6 = (bf16[32,128]{1,0:T(8,128)(2,1)S(1)}, bf16[32,128]{1,0:T(8,128)(2,1)S(1)}, u32[]{:S(2)}, u32[]{:S(2)}) collective-permute-start(bf16[32,128]{1,0:T(8,128)(2,1)S(1)} %plane_sum.1.part_ref.refs_0_), channel_id=1, source_target_pairs={{4,0},{68,64},{5,1},{69,65},{12,8},{76,72},{13,9},{77,73},{20,16},... | collective-permute-start | bytes 24584 | tf_op jit(solution)/shard_map/ppermute | solution.py:247
  43.9 0.0 collective-permute-done.2.side_ref
  43.9 1.3 %collective-permute-start.5 = (bf16[32,128]{1,0:T(8,128)(2,1)S(1)}, bf16[32,128]{1,0:T(8,128)(2,1)S(1)}, u32[]{:S(2)}, u32[]{:S(2)}) collective-permute-start(bf16[32,128]{1,0:T(8,128)(2,1)S(1)} %side_sum.1), channel_id=1, source_target_pairs={{6,64},{2,0},{7,65},{3,1},{14,72},{10,8},{15,73},{11,9},{22,80},{1... | collective-permute-start | bytes 24584 | tf_op jit(solution)/shard_map/ppermute | solution.py:247
  45.2 1.3 %collective-permute-start.4 = (bf16[32,128]{1,0:T(8,128)(2,1)S(1)}, bf16[32,128]{1,0:T(8,128)(2,1)S(1)}, u32[]{:S(2)}, u32[]{:S(2)}) collective-permute-start(bf16[32,128]{1,0:T(8,128)(2,1)S(1)} %side_sum.1), channel_id=1, source_target_pairs={{6,0},{2,64},{7,1},{3,65},{14,8},{10,72},{15,9},{11,73},{22,16},{1... | collective-permute-start | bytes 24584 | tf_op jit(solution)/shard_map/ppermute | solution.py:247
  46.5 4.8 %collective-permute-start.3 = (bf16[32,128]{1,0:T(8,128)(2,1)S(1)}, bf16[32,128]{1,0:T(8,128)(2,1)S(1)}, u32[]{:S(2)}, u32[]{:S(2)}) collective-permute-start(bf16[32,128]{1,0:T(8,128)(2,1)S(1)} %side_sum.1), channel_id=1, source_target_pairs={{64,0},{0,64},{65,1},{1,65},{72,8},{8,72},{73,9},{9,73},{80,16},{1... | collective-permute-start | bytes 24584 | tf_op jit(solution)/shard_map/ppermute | solution.py:247
  51.3 3.9 %collective-permute-done.7.refs_5_ = bf16[32,128]{1,0:T(8,128)(2,1)S(1)} collective-permute-done((bf16[32,128]{1,0:T(8,128)(2,1)S(1)}, bf16[32,128]{1,0:T(8,128)(2,1)S(1)}, u32[]{:S(2)}, u32[]{:S(2)}) %collective-permute-start.7) | collective-permute-done | bytes 8224 | tf_op jit(solution)/shard_map/ppermute | solution.py:247
  55.2 1.3 %collective-permute-done.6.refs_4_ = bf16[32,128]{1,0:T(8,128)(2,1)S(1)} collective-permute-done((bf16[32,128]{1,0:T(8,128)(2,1)S(1)}, bf16[32,128]{1,0:T(8,128)(2,1)S(1)}, u32[]{:S(2)}, u32[]{:S(2)}) %collective-permute-start.6) | collective-permute-done | bytes 8224 | tf_op jit(solution)/shard_map/ppermute | solution.py:247
  56.5 0.0 collective-permute-done.5.refs_3_
  56.5 1.2 %collective-permute-done.4.refs_2_ = bf16[32,128]{1,0:T(8,128)(2,1)S(1)} collective-permute-done((bf16[32,128]{1,0:T(8,128)(2,1)S(1)}, bf16[32,128]{1,0:T(8,128)(2,1)S(1)}, u32[]{:S(2)}, u32[]{:S(2)}) %collective-permute-start.4) | collective-permute-done | bytes 8224 | tf_op jit(solution)/shard_map/ppermute | solution.py:247
  57.7 0.0 collective-permute-done.3.refs_1_
  57.7 1.3 %collective-permute-start.9 = (bf16[32,128]{1,0:T(8,128)(2,1)S(1)}, bf16[32,128]{1,0:T(8,128)(2,1)S(1)}, u32[]{:S(2)}, u32[]{:S(2)}) collective-permute-start(bf16[32,128]{1,0:T(8,128)(2,1)S(1)} %depth_sum.1), channel_id=1, source_target_pairs={{0,2},{64,66},{1,3},{65,67},{8,10},{72,74},{9,11},{73,75},{16,18},... | collective-permute-start | bytes 24584 | tf_op jit(solution)/shard_map/ppermute | solution.py:247
  59.0 0.7 collective-permute-start.8
  59.7 0.1 collective-permute-done.9
  59.8 0.0 collective-permute-done.8
  59.8 0.7 collective-permute-start.10
  60.4 0.0 collective-permute-done.10.two_ref
  60.5 19.1 %all_to_all.11 = bf16[64,32,128]{2,1,0:T(8,128)(2,1)S(1)} all-to-all(bf16[64,32,128]{2,1,0:T(8,128)(2,1)S(1)} %copies.1), channel_id=1, replica_groups={{289,288,297,296,305,304,313,312,257,256,265,264,273,272,281,280,417,41..., dimensions={0} | all-to-all | bytes 1048576 | tf_op jit(solution)/shard_map/all_to_all | solution.py:372
  79.6 1.3 %unpack.1 = (f32[2592,96]{1,0:T(8,128)}, f32[96]{0:T(128)}, f32[3,27,96]{2,1,0:T(8,128)}, f32[3]{0:T(128)}) custom-call(bf16[2048,128]{1,0:T(8,128)(2,1)S(1)} %bitcast.17), custom_call_target="tpu_custom_call" | custom-call | tf_op jit(solution)/shard_map/unpack/pallas_call | solution.py:374
  (7 shorter events, 0.1 us)
Async XLA Ops:
  0.6 9.4 %copy-start = (bf16[27,96,3]{1,0,2:T(8,128)(2,1)S(1)}, bf16[27,96,3]{1,0,2:T(8,128)(2,1)}, u32[]{:S(2)}) copy-start(bf16[27,96,3]{1,0,2:T(8,128)(2,1)} %param.9) | copy-start | bytes 46660
  1.6 8.4 %collective-permute-start.1 = (bf16[5,2,96,128]{3,2,1,0:T(8,128)(2,1)S(1)}, bf16[5,2,96,128]{3,2,1,0:T(8,128)(2,1)S(1)}, u32[]{:S(2)}, u32[]{:S(2)}) collective-permute-start(bf16[5,2,96,128]{3,2,1,0:T(8,128)(2,1)S(1)} %bitcast.19), channel_id=1, source_target_pairs={{8,16},{16,8},{24,32},{32,24},{40,48},{48,40},{56,64},{64,56},{72,... | collective-permute-start | bytes 737288 | tf_op jit(solution)/shard_map/ppermute | solution.py:340
  5.7 4.4 %collective-permute-start = (bf16[5,2,96,128]{3,2,1,0:T(8,128)(2,1)S(1)}, bf16[5,2,96,128]{3,2,1,0:T(8,128)(2,1)S(1)}, u32[]{:S(2)}, u32[]{:S(2)}) collective-permute-start(bf16[5,2,96,128]{3,2,1,0:T(8,128)(2,1)S(1)} %bitcast.20), channel_id=1, source_target_pairs={{0,8},{8,0},{16,24},{24,16},{32,40},{40,32},{48,56},{56,48},{64,72... | collective-permute-start | bytes 737288 | tf_op jit(solution)/shard_map/ppermute | solution.py:339
  40.6 3.3 %collective-permute-start.2 = (bf16[32,128]{1,0:T(8,128)(2,1)S(1)}, bf16[32,128]{1,0:T(8,128)(2,1)S(1)}, u32[]{:S(2)}, u32[]{:S(2)}) collective-permute-start(bf16[32,128]{1,0:T(8,128)(2,1)S(1)} %plane_sum.1.part_ref.refs_0_), channel_id=1, source_target_pairs={{70,6},{66,2},{71,7},{67,3},{78,14},{74,10},{79,15},{75,11},{86,22... | collective-permute-start | bytes 24584 | tf_op jit(solution)/shard_map/ppermute | solution.py:247
  41.3 13.9 %collective-permute-start.7 = (bf16[32,128]{1,0:T(8,128)(2,1)S(1)}, bf16[32,128]{1,0:T(8,128)(2,1)S(1)}, u32[]{:S(2)}, u32[]{:S(2)}) collective-permute-start(bf16[32,128]{1,0:T(8,128)(2,1)S(1)} %plane_sum.1.part_ref.refs_0_), channel_id=1, source_target_pairs={{68,0},{4,64},{69,1},{5,65},{76,8},{12,72},{77,9},{13,73},{84,16},... | collective-permute-start | bytes 24584 | tf_op jit(solution)/shard_map/ppermute | solution.py:247
  42.6 13.9 %collective-permute-start.6 = (bf16[32,128]{1,0:T(8,128)(2,1)S(1)}, bf16[32,128]{1,0:T(8,128)(2,1)S(1)}, u32[]{:S(2)}, u32[]{:S(2)}) collective-permute-start(bf16[32,128]{1,0:T(8,128)(2,1)S(1)} %plane_sum.1.part_ref.refs_0_), channel_id=1, source_target_pairs={{4,0},{68,64},{5,1},{69,65},{12,8},{76,72},{13,9},{77,73},{20,16},... | collective-permute-start | bytes 24584 | tf_op jit(solution)/shard_map/ppermute | solution.py:247
  43.9 12.6 %collective-permute-start.5 = (bf16[32,128]{1,0:T(8,128)(2,1)S(1)}, bf16[32,128]{1,0:T(8,128)(2,1)S(1)}, u32[]{:S(2)}, u32[]{:S(2)}) collective-permute-start(bf16[32,128]{1,0:T(8,128)(2,1)S(1)} %side_sum.1), channel_id=1, source_target_pairs={{6,64},{2,0},{7,65},{3,1},{14,72},{10,8},{15,73},{11,9},{22,80},{1... | collective-permute-start | bytes 24584 | tf_op jit(solution)/shard_map/ppermute | solution.py:247
  45.2 12.5 %collective-permute-start.4 = (bf16[32,128]{1,0:T(8,128)(2,1)S(1)}, bf16[32,128]{1,0:T(8,128)(2,1)S(1)}, u32[]{:S(2)}, u32[]{:S(2)}) collective-permute-start(bf16[32,128]{1,0:T(8,128)(2,1)S(1)} %side_sum.1), channel_id=1, source_target_pairs={{6,0},{2,64},{7,1},{3,65},{14,8},{10,72},{15,9},{11,73},{22,16},{1... | collective-permute-start | bytes 24584 | tf_op jit(solution)/shard_map/ppermute | solution.py:247
  46.5 11.2 %collective-permute-start.3 = (bf16[32,128]{1,0:T(8,128)(2,1)S(1)}, bf16[32,128]{1,0:T(8,128)(2,1)S(1)}, u32[]{:S(2)}, u32[]{:S(2)}) collective-permute-start(bf16[32,128]{1,0:T(8,128)(2,1)S(1)} %side_sum.1), channel_id=1, source_target_pairs={{64,0},{0,64},{65,1},{1,65},{72,8},{8,72},{73,9},{9,73},{80,16},{1... | collective-permute-start | bytes 24584 | tf_op jit(solution)/shard_map/ppermute | solution.py:247
  57.7 2.1 %collective-permute-start.9 = (bf16[32,128]{1,0:T(8,128)(2,1)S(1)}, bf16[32,128]{1,0:T(8,128)(2,1)S(1)}, u32[]{:S(2)}, u32[]{:S(2)}) collective-permute-start(bf16[32,128]{1,0:T(8,128)(2,1)S(1)} %depth_sum.1), channel_id=1, source_target_pairs={{0,2},{64,66},{1,3},{65,67},{8,10},{72,74},{9,11},{73,75},{16,18},... | collective-permute-start | bytes 24584 | tf_op jit(solution)/shard_map/ppermute | solution.py:247
  59.0 0.8 collective-permute-start.8
  59.8 0.7 collective-permute-start.10

commit v9 on v8

--- a/solution.py
+++ b/solution.py
@@ -29,7 +29,7 @@
 EDGE_AXES = ("x", "z1", "z0", "y")
 NEAR = ("x", "z0", "y", "c")
 DEPTH = ("zh", "z1")
-FAR = (((5, 0), (4, 1)), ((4, 0), (5, 1)))
+FAR = (((4, 0), (5, 1)), ((5, 0), (4, 1)))
 SIDE = ((7, 6), (3, 2))
 CLOSE = (((6, 1), (2, 0)), ((6, 0), (2, 1)), ((1, 0), (0, 1)))
 SPREAD = (((1, 7),), ((0, 2), (1, 3)), ((2, 4), (3, 5), (7, 6)))
@@ -55,7 +55,7 @@
     return jnp.where(lane > 0, pltpu.roll(v, 1, 1), 0.0)
 
 
-FIRST = 41
+FIRST = 43
 
 
 def scatter_groups():

time: 81.6 us -> 81.5 us (level)
  no operation moved by 1% of the time
where the time goes in v9:
time: 81.5 us; the launch traced here: 80.9 us
  blocking collectives  44.6 us (55%)
  starting transfers between devices  17.3 us (21%)
  waiting for transfers between devices  7.1 us (9%)
  Pallas kernels  6.42 us (8%)
  local copies, waits for them, and re-layouts  4.62 us (6%)
  between operations  0.83 us (1%)
    all_to_all x1, blocking collectives, local(): lax.all_to_all(packed.reshape(near, chunk, W), AXES, 0, 0, axis_index_gro...  26.2 us
    all_to_all x1, blocking collectives, local(): lax.all_to_all(parts, AXES, 0, 0, axis_index_groups=scatter_groups())  18.4 us
    ppermute x9, starting transfers between devices, pass_on(): lax.ppermute(value, DEPTH[::-1], [(place[i], place[j]) for i, j in pairs])  12.6 us
    ppermute x9, waiting for transfers between devices, pass_on(): lax.ppermute(value, DEPTH[::-1], [(place[i], place[j]) for i, j in pairs])  7.09 us
    pallas_call x1, Pallas kernels, local(): k1_call(n_rows, scale)(own, one, two, wt, conv_bias[:, None], wo, ob, tgt)  4.91 us
    ppermute x1, starting transfers between devices, local(): lax.ppermute(own, axes, [(2 * i, 2 * j) for i, j in odd] + [(2 * i + 1, 2...  4.03 us
  transfers between devices with their start and end apart: 11, of which 4 were waited for; matrix products, arithmetic and copies ran while one was open for 4% of the time, Pallas kernels for 0%

profile of v9, /device:TPU:1, one launch (start us, length us, event | category | flops | bytes accessed | tf_op | source)
XLA Modules:
  0.0 80.9 jit_solution(3367629670467077504)
XLA Ops:
  0.6 0.0 copy-start
  0.6 1.0 %copy.16 = bf16[1,96,5,2,128]{4,1,3,2,0:T(8,128)(2,1)S(1)} copy(bf16[1,96,5,2,128]{4,3,2,1,0:T(2,128)(2,1)} %param.6) | data formatting | bytes 491520 | tf_op args[0]
  1.6 4.0 %collective-permute-start.1 = (bf16[5,2,96,128]{3,2,1,0:T(8,128)(2,1)S(1)}, bf16[5,2,96,128]{3,2,1,0:T(8,128)(2,1)S(1)}, u32[]{:S(2)}, u32[]{:S(2)}) collective-permute-start(bf16[5,2,96,128]{3,2,1,0:T(8,128)(2,1)S(1)} %bitcast.19), channel_id=1, source_target_pairs={{8,16},{16,8},{24,32},{32,24},{40,48},{48,40},{56,64},{64,56},{72,... | collective-permute-start | bytes 737288 | tf_op jit(solution)/shard_map/ppermute | solution.py:340
  5.7 0.7 collective-permute-start
  6.4 0.7 copy.13
  7.1 0.7 convert_element_type.10
  7.8 0.8 copy.14.cb_ref
  8.6 1.4 %copy.12 = bf16[3,864,96]{1,2,0:T(8,128)(2,1)S(1)} copy(bf16[3,864,96]{2,1,0:T(8,128)(2,1)} %bitcast.24) | data formatting | bytes 995328 | tf_op jit(solution)/shard_map/reshape | solution.py:342
  10.0 0.0 copy-done
  10.0 0.0 collective-permute-done.1.two_ref
  10.0 0.0 collective-permute-done.one_ref
  10.0 4.9 %device_part.1 = (bf16[1,3,5,2,128]{4,3,2,1,0:T(2,128)(2,1)}, bf16[2048,128]{1,0:T(8,128)(2,1)S(1)}) custom-call(bf16[5,2,96,128]{3,2,1,0:T(8,128)(2,1)S(1)} %bitcast.21, bf16[5,2,96,128]{3,2,1,0:T(8,128)(2,1)S(1)} %collective-permute-done.one_ref, bf16[5,2,96,128]{3,2,1,0:T(8,128)(2,1)S(1)} %collective-permute-done.1.two_ref, ...), custom_call_target="tpu_custom_call" | custom-call | tf_op jit(solution)/shard_map/device_part/pallas_call | solution.py:347
  15.0 26.2 %all_to_all.10.in_ref = bf16[64,32,128]{2,1,0:T(8,128)(2,1)S(1)} all-to-all(bf16[64,32,128]{2,1,0:T(8,128)(2,1)S(1)} %bitcast.22), channel_id=1, replica_groups={{297,296,289,288,313,312,305,304,265,264,257,256,281,280,273,272,425,42..., dimensions={0} | all-to-all | bytes 1048576 | tf_op jit(solution)/shard_map/all_to_all | solution.py:361
  41.1 0.1 plane_sum.1.part_ref.refs_0_
  41.2 0.7 collective-permute-start.2
  41.9 1.3 %collective-permute-start.7 = (bf16[32,128]{1,0:T(8,128)(2,1)S(1)}, bf16[32,128]{1,0:T(8,128)(2,1)S(1)}, u32[]{:S(2)}, u32[]{:S(2)}) collective-permute-start(bf16[32,128]{1,0:T(8,128)(2,1)S(1)} %plane_sum.1.part_ref.refs_0_), channel_id=1, source_target_pairs={{4,0},{68,64},{5,1},{69,65},{12,8},{76,72},{13,9},{77,73},{20,16},... | collective-permute-start | bytes 24584 | tf_op jit(solution)/shard_map/ppermute | solution.py:247
  43.2 1.3 %collective-permute-start.6 = (bf16[32,128]{1,0:T(8,128)(2,1)S(1)}, bf16[32,128]{1,0:T(8,128)(2,1)S(1)}, u32[]{:S(2)}, u32[]{:S(2)}) collective-permute-start(bf16[32,128]{1,0:T(8,128)(2,1)S(1)} %plane_sum.1.part_ref.refs_0_), channel_id=1, source_target_pairs={{68,0},{4,64},{69,1},{5,65},{76,8},{12,72},{77,9},{13,73},{84,16},... | collective-permute-start | bytes 24584 | tf_op jit(solution)/shard_map/ppermute | solution.py:247
  44.5 0.0 collective-permute-done.2.side_ref
  44.5 1.3 %collective-permute-start.5 = (bf16[32,128]{1,0:T(8,128)(2,1)S(1)}, bf16[32,128]{1,0:T(8,128)(2,1)S(1)}, u32[]{:S(2)}, u32[]{:S(2)}) collective-permute-start(bf16[32,128]{1,0:T(8,128)(2,1)S(1)} %side_sum.1), channel_id=1, source_target_pairs={{6,64},{2,0},{7,65},{3,1},{14,72},{10,8},{15,73},{11,9},{22,80},{1... | collective-permute-start | bytes 24584 | tf_op jit(solution)/shard_map/ppermute | solution.py:247
  45.8 1.3 %collective-permute-start.4 = (bf16[32,128]{1,0:T(8,128)(2,1)S(1)}, bf16[32,128]{1,0:T(8,128)(2,1)S(1)}, u32[]{:S(2)}, u32[]{:S(2)}) collective-permute-start(bf16[32,128]{1,0:T(8,128)(2,1)S(1)} %side_sum.1), channel_id=1, source_target_pairs={{6,0},{2,64},{7,1},{3,65},{14,8},{10,72},{15,9},{11,73},{22,16},{1... | collective-permute-start | bytes 24584 | tf_op jit(solution)/shard_map/ppermute | solution.py:247
  47.1 4.2 %collective-permute-start.3 = (bf16[32,128]{1,0:T(8,128)(2,1)S(1)}, bf16[32,128]{1,0:T(8,128)(2,1)S(1)}, u32[]{:S(2)}, u32[]{:S(2)}) collective-permute-start(bf16[32,128]{1,0:T(8,128)(2,1)S(1)} %side_sum.1), channel_id=1, source_target_pairs={{64,0},{0,64},{65,1},{1,65},{72,8},{8,72},{73,9},{9,73},{80,16},{1... | collective-permute-start | bytes 24584 | tf_op jit(solution)/shard_map/ppermute | solution.py:247
  51.3 4.0 %collective-permute-done.7.refs_5_ = bf16[32,128]{1,0:T(8,128)(2,1)S(1)} collective-permute-done((bf16[32,128]{1,0:T(8,128)(2,1)S(1)}, bf16[32,128]{1,0:T(8,128)(2,1)S(1)}, u32[]{:S(2)}, u32[]{:S(2)}) %collective-permute-start.7) | collective-permute-done | bytes 8224 | tf_op jit(solution)/shard_map/ppermute | solution.py:247
  55.3 1.2 %collective-permute-done.6.refs_4_ = bf16[32,128]{1,0:T(8,128)(2,1)S(1)} collective-permute-done((bf16[32,128]{1,0:T(8,128)(2,1)S(1)}, bf16[32,128]{1,0:T(8,128)(2,1)S(1)}, u32[]{:S(2)}, u32[]{:S(2)}) %collective-permute-start.6) | collective-permute-done | bytes 8224 | tf_op jit(solution)/shard_map/ppermute | solution.py:247
  56.5 0.0 collective-permute-done.5.refs_3_
  56.5 1.8 %collective-permute-done.4.refs_2_ = bf16[32,128]{1,0:T(8,128)(2,1)S(1)} collective-permute-done((bf16[32,128]{1,0:T(8,128)(2,1)S(1)}, bf16[32,128]{1,0:T(8,128)(2,1)S(1)}, u32[]{:S(2)}, u32[]{:S(2)}) %collective-permute-start.4) | collective-permute-done | bytes 8224 | tf_op jit(solution)/shard_map/ppermute | solution.py:247
  58.3 0.0 collective-permute-done.3.refs_1_
  58.3 1.3 %collective-permute-start.9 = (bf16[32,128]{1,0:T(8,128)(2,1)S(1)}, bf16[32,128]{1,0:T(8,128)(2,1)S(1)}, u32[]{:S(2)}, u32[]{:S(2)}) collective-permute-start(bf16[32,128]{1,0:T(8,128)(2,1)S(1)} %depth_sum.1), channel_id=1, source_target_pairs={{0,2},{64,66},{1,3},{65,67},{8,10},{72,74},{9,11},{73,75},{16,18},... | collective-permute-start | bytes 24584 | tf_op jit(solution)/shard_map/ppermute | solution.py:247
  59.6 0.7 collective-permute-start.8
  60.3 0.1 collective-permute-done.9
  60.4 0.0 collective-permute-done.8
  60.4 0.7 collective-permute-start.10
  61.1 0.0 collective-permute-done.10.two_ref
  61.1 18.4 %all_to_all.11 = bf16[64,32,128]{2,1,0:T(8,128)(2,1)S(1)} all-to-all(bf16[64,32,128]{2,1,0:T(8,128)(2,1)S(1)} %copies.1), channel_id=1, replica_groups={{297,296,289,288,313,312,305,304,265,264,257,256,281,280,273,272,425,42..., dimensions={0} | all-to-all | bytes 1048576 | tf_op jit(solution)/shard_map/all_to_all | solution.py:372
  79.6 1.3 %unpack.1 = (f32[2592,96]{1,0:T(8,128)}, f32[96]{0:T(128)}, f32[3,27,96]{2,1,0:T(8,128)}, f32[3]{0:T(128)}) custom-call(bf16[2048,128]{1,0:T(8,128)(2,1)S(1)} %bitcast.17), custom_call_target="tpu_custom_call" | custom-call | tf_op jit(solution)/shard_map/unpack/pallas_call | solution.py:374
  (7 shorter events, 0.1 us)
Async XLA Ops:
  0.6 9.4 %copy-start = (bf16[27,96,3]{1,0,2:T(8,128)(2,1)S(1)}, bf16[27,96,3]{1,0,2:T(8,128)(2,1)}, u32[]{:S(2)}) copy-start(bf16[27,96,3]{1,0,2:T(8,128)(2,1)} %param.9) | copy-start | bytes 46660
  1.6 8.4 %collective-permute-start.1 = (bf16[5,2,96,128]{3,2,1,0:T(8,128)(2,1)S(1)}, bf16[5,2,96,128]{3,2,1,0:T(8,128)(2,1)S(1)}, u32[]{:S(2)}, u32[]{:S(2)}) collective-permute-start(bf16[5,2,96,128]{3,2,1,0:T(8,128)(2,1)S(1)} %bitcast.19), channel_id=1, source_target_pairs={{8,16},{16,8},{24,32},{32,24},{40,48},{48,40},{56,64},{64,56},{72,... | collective-permute-start | bytes 737288 | tf_op jit(solution)/shard_map/ppermute | solution.py:340
  5.7 4.4 %collective-permute-start = (bf16[5,2,96,128]{3,2,1,0:T(8,128)(2,1)S(1)}, bf16[5,2,96,128]{3,2,1,0:T(8,128)(2,1)S(1)}, u32[]{:S(2)}, u32[]{:S(2)}) collective-permute-start(bf16[5,2,96,128]{3,2,1,0:T(8,128)(2,1)S(1)} %bitcast.20), channel_id=1, source_target_pairs={{0,8},{8,0},{16,24},{24,16},{32,40},{40,32},{48,56},{56,48},{64,72... | collective-permute-start | bytes 737288 | tf_op jit(solution)/shard_map/ppermute | solution.py:339
  41.2 3.3 %collective-permute-start.2 = (bf16[32,128]{1,0:T(8,128)(2,1)S(1)}, bf16[32,128]{1,0:T(8,128)(2,1)S(1)}, u32[]{:S(2)}, u32[]{:S(2)}) collective-permute-start(bf16[32,128]{1,0:T(8,128)(2,1)S(1)} %plane_sum.1.part_ref.refs_0_), channel_id=1, source_target_pairs={{70,6},{66,2},{71,7},{67,3},{78,14},{74,10},{79,15},{75,11},{86,22... | collective-permute-start | bytes 24584 | tf_op jit(solution)/shard_map/ppermute | solution.py:247
  41.9 13.5 %collective-permute-start.7 = (bf16[32,128]{1,0:T(8,128)(2,1)S(1)}, bf16[32,128]{1,0:T(8,128)(2,1)S(1)}, u32[]{:S(2)}, u32[]{:S(2)}) collective-permute-start(bf16[32,128]{1,0:T(8,128)(2,1)S(1)} %plane_sum.1.part_ref.refs_0_), channel_id=1, source_target_pairs={{4,0},{68,64},{5,1},{69,65},{12,8},{76,72},{13,9},{77,73},{20,16},... | collective-permute-start | bytes 24584 | tf_op jit(solution)/shard_map/ppermute | solution.py:247
  43.2 13.3 %collective-permute-start.6 = (bf16[32,128]{1,0:T(8,128)(2,1)S(1)}, bf16[32,128]{1,0:T(8,128)(2,1)S(1)}, u32[]{:S(2)}, u32[]{:S(2)}) collective-permute-start(bf16[32,128]{1,0:T(8,128)(2,1)S(1)} %plane_sum.1.part_ref.refs_0_), channel_id=1, source_target_pairs={{68,0},{4,64},{69,1},{5,65},{76,8},{12,72},{77,9},{13,73},{84,16},... | collective-permute-start | bytes 24584 | tf_op jit(solution)/shard_map/ppermute | solution.py:247
  44.5 12.0 %collective-permute-start.5 = (bf16[32,128]{1,0:T(8,128)(2,1)S(1)}, bf16[32,128]{1,0:T(8,128)(2,1)S(1)}, u32[]{:S(2)}, u32[]{:S(2)}) collective-permute-start(bf16[32,128]{1,0:T(8,128)(2,1)S(1)} %side_sum.1), channel_id=1, source_target_pairs={{6,64},{2,0},{7,65},{3,1},{14,72},{10,8},{15,73},{11,9},{22,80},{1... | collective-permute-start | bytes 24584 | tf_op jit(solution)/shard_map/ppermute | solution.py:247
  45.8 12.5 %collective-permute-start.4 = (bf16[32,128]{1,0:T(8,128)(2,1)S(1)}, bf16[32,128]{1,0:T(8,128)(2,1)S(1)}, u32[]{:S(2)}, u32[]{:S(2)}) collective-permute-start(bf16[32,128]{1,0:T(8,128)(2,1)S(1)} %side_sum.1), channel_id=1, source_target_pairs={{6,0},{2,64},{7,1},{3,65},{14,8},{10,72},{15,9},{11,73},{22,16},{1... | collective-permute-start | bytes 24584 | tf_op jit(solution)/shard_map/ppermute | solution.py:247
  47.1 11.2 %collective-permute-start.3 = (bf16[32,128]{1,0:T(8,128)(2,1)S(1)}, bf16[32,128]{1,0:T(8,128)(2,1)S(1)}, u32[]{:S(2)}, u32[]{:S(2)}) collective-permute-start(bf16[32,128]{1,0:T(8,128)(2,1)S(1)} %side_sum.1), channel_id=1, source_target_pairs={{64,0},{0,64},{65,1},{1,65},{72,8},{8,72},{73,9},{9,73},{80,16},{1... | collective-permute-start | bytes 24584 | tf_op jit(solution)/shard_map/ppermute | solution.py:247
  58.3 2.1 %collective-permute-start.9 = (bf16[32,128]{1,0:T(8,128)(2,1)S(1)}, bf16[32,128]{1,0:T(8,128)(2,1)S(1)}, u32[]{:S(2)}, u32[]{:S(2)}) collective-permute-start(bf16[32,128]{1,0:T(8,128)(2,1)S(1)} %depth_sum.1), channel_id=1, source_target_pairs={{0,2},{64,66},{1,3},{65,67},{8,10},{72,74},{9,11},{73,75},{16,18},... | collective-permute-start | bytes 24584 | tf_op jit(solution)/shard_map/ppermute | solution.py:247
  59.6 0.8 collective-permute-start.8
  60.4 0.7 collective-permute-start.10
